TPU v7x, 256 devices: a whole 4x4x8 slice. The times are simulated.
256 devices in a mesh: ctx: 64 (over x, z, core), head: 4 (over y).
Axes of the slice: x: 4, y: 4, z: 8, core: 2. Of those that a mesh axis runs over, the one named last changes fastest.
Arguments:
- queries: bfloat16 [16384, 2560], P('ctx', 'head'), may hold values from -8 to 8
- key_tokens: bfloat16 [16384, 2560], P('ctx', 'head'), may hold values from -8 to 8
- value_tokens: bfloat16 [16384, 2560], P('ctx', 'head'), may hold values from -8 to 8
- pair_keys: int32 [512, 4], P('ctx'), may hold values from 0 to 511, as said below
- pair_count: int32 [512], P('ctx'), may hold values from 1 to 4, as said below
Outputs:
- attended: bfloat16 [16384, 2560], P('ctx', 'head')
Inputs may be any that keep to these rules, and one draw needn't show every extreme that they name: `pair_keys`: the 4 entries of a row are distinct, padded slots too. Key block c lies on index c // 8 of ctx. Among all 4 slots (padded ones included) of the 8 rows of one index of ctx, at most 2 name key blocks of any one index, its own included, and on every index some one index is named exactly 2 times. `pair_count`: every index of ctx has a query block whose count is 4.
All inputs are finite; a program needn't handle non-finite values.
Results may differ from a plain program's by a relative error of at most 0.0059.
Values may be sent and summed in bfloat16 or wider, within the bound.
No kernel may reach another device: no remote copies, remote signals or barrier semaphores. Data moves between devices by JAX's collectives and lax.ppermute only.
A program may use at most 128 MiB of HBM per device.

v0:
```python
import functools
import math

import jax
import jax.numpy as jnp
from jax import lax
from jax.experimental import pallas as pl
from jax.experimental.pallas import tpu as pltpu
from jax.sharding import PartitionSpec as P

HD = 128
BLOCK = 32
NX, NZ, NC = 4, 8, 2
BLOCKS = 8
SLOTS = 4
TOKENS = BLOCKS * BLOCK
HALF = TOKENS // 2
REQUEST = 16
STATS = 32
MEANS = 16
PLANE = NX * NC
MOST = 2 * PLANE
FIRST = 2
CHUNK = 4
NEGATIVE = -1e30
ROWS_ROWS = (((1,), (1,)), ((), ()))
COLS_COLS = (((0,), (0,)), ((), ()))
PARAMS = pltpu.CompilerParams(vmem_limit_bytes=24 * 1024 * 1024)


def move(array, dx=0, dz=0, dc=0):
    pairs = []
    for x in range(NX):
        for z in range(NZ):
            for c in range(NC):
                to = (((x + dx) % NX) * NZ + (z + dz) % NZ) * NC + (c ^ dc)
                pairs.append(((x * NZ + z) * NC + c, to))
    return lax.ppermute(array, "ctx", pairs)


def iota(shape, axis):
    return lax.broadcasted_iota(jnp.int32, shape, axis)


def part_kernel(heads, groups, pos_ref, *rest):
    count = len(groups)
    q_refs, rest = rest[:count], rest[count:]
    key_refs, rest = rest[:PLANE], rest[PLANE:]
    value_refs, rest = rest[:PLANE], rest[PLANE:]
    out_refs, rest = rest[:count], rest[count:]
    bufs, rest = rest[:count], rest[count:]
    accs, rest = rest[:count], rest[count:]
    tops, rest = rest[:count], rest[count:]
    sums, rest = rest[:count], rest[count:]
    biases, rest = rest[:count], rest[count:]
    means, ids_vmem, ids_ref, slot_b, slot_k, k_sem, v_sem, mean_sem, ids_sem = rest
    mx, mz, mc = pos_ref[0], pos_ref[1], pos_ref[2]
    inv_root = 1.0 / math.sqrt(HD)

    def copies(g, i, within, n):
        first = pl.multiple_of(within * BLOCK, BLOCK)
        value_first = value_refs[i].shape[0] - TOKENS + first
        return (
            pltpu.make_async_copy(
                key_refs[i].at[pl.ds(first, BLOCK)], bufs[g].at[n, pl.ds(0, BLOCK)], k_sem.at[g, n]
            ),
            pltpu.make_async_copy(
                value_refs[i].at[pl.ds(pl.multiple_of(value_first, 16), BLOCK)],
                bufs[g].at[n, pl.ds(BLOCK, BLOCK)],
                v_sem.at[g, n],
            ),
        )

    ids_copies = []
    for g, (_, _, _, place) in enumerate(groups):
        asked = q_refs[g][place : place + REQUEST, :HD].astype(jnp.float32)
        ids_vmem[g] = asked[:BLOCKS].astype(jnp.int32)
        ids_copies.append(pltpu.make_async_copy(ids_vmem.at[g], ids_ref.at[g], ids_sem.at[g]))
        ids_copies[g].start()
    mean_copies = []
    for i in range(PLANE):
        source = key_refs[i].at[pl.ds(TOKENS, MEANS)]
        mean_copies.append(pltpu.make_async_copy(source, means.at[i], mean_sem.at[i]))
        mean_copies[i].start()
    for copy in ids_copies:
        copy.wait()

    useds = []
    for g, (_, low, blocks, _) in enumerate(groups):

        def ask(b, n, g=g):
            limit = ids_ref[g, b, 2 * SLOTS]
            for p in range(SLOTS):
                owner = ids_ref[g, b, p]
                here = (p < limit) & (((owner >> 1) & (NZ - 1)) == mz)

                @pl.when(here)
                def _(n=n, p=p, owner=owner):
                    within = ids_ref[g, b, SLOTS + p]
                    rel = (((owner >> 4) - mx) & (NX - 1)) * NC + ((owner & 1) ^ mc)
                    slot_b[g, n] = b
                    slot_k[g, n] = rel * BLOCKS + within
                    for i in range(PLANE):

                        @pl.when(rel == i)
                        def _(i=i):
                            for copy in copies(g, i, within, n):
                                copy.start()

                n = n + here.astype(jnp.int32)
            return n

        useds.append(lax.fori_loop(low, low + blocks, ask, jnp.int32(0)))

    def arrived(g, n):
        @pl.when(n < useds[g])
        def _():
            for copy in copies(g, 0, 0, n):
                copy.wait()

    def q_of(g, cols):
        pieces = [q_refs[g][row : row + HALF, cols] for row in groups[g][0]]
        return pieces[0] if len(pieces) == 1 else jnp.concatenate(pieces, axis=0)

    chunks = []
    for g, (_, low, blocks, _) in enumerate(groups):
        tokens = blocks * BLOCK
        used = useds[g]
        chunks.append((jnp.maximum(used - FIRST, 0) + CHUNK - 1) // CHUNK)

        def blank(n, carry, g=g):
            slot_b[g, n] = -1
            bufs[g][n] = jnp.zeros(bufs[g].shape[1:], bufs[g].dtype)
            return carry

        lax.fori_loop(used, FIRST + CHUNK * chunks[g], blank, 0)
        shape = (PLANE * BLOCKS, tokens)
        key_ids, token_blocks = iota(shape, 0), iota(shape, 1) // BLOCK + low

        def exclude(n, table, g=g, key_ids=key_ids, token_blocks=token_blocks):
            hit = (key_ids == slot_k[g, n]) & (token_blocks == slot_b[g, n])
            return jnp.where(hit, NEGATIVE, table)

        bias = jnp.full(shape, math.log(BLOCK), jnp.float32)
        biases[g][...] = lax.fori_loop(0, used, exclude, bias)

    def slot_bias(g, n):
        _, low, blocks, _ = groups[g]
        token_blocks = iota((1, blocks * BLOCK), 1) // BLOCK + low
        return jnp.where(token_blocks == slot_b[g, n], 0.0, NEGATIVE)

    for copy in mean_copies:
        copy.wait()
    mean_tiles = []
    for h in range(heads):
        tiles = [means[i, :, pl.ds(h * HD, HD)].astype(jnp.float32) for i in range(PLANE)]
        both = [[t[:BLOCKS] for t in tiles], [t[BLOCKS:] for t in tiles]]
        mean_tiles.append([jnp.concatenate(b, axis=0).astype(jnp.bfloat16) for b in both])

    for g in range(count):
        for j in range(FIRST):
            arrived(g, j)
        slot_rows = [slot_bias(g, j) for j in range(FIRST)]
        tokens = groups[g][2] * BLOCK
        for h in range(heads):
            cols = pl.ds(h * HD, HD)
            keys = [mean_tiles[h][0]] + [bufs[g][j, :BLOCK, cols] for j in range(FIRST)]
            values = [mean_tiles[h][1]] + [bufs[g][j, BLOCK:, cols] for j in range(FIRST)]
            logits = lax.dot_general(
                jnp.concatenate(keys, axis=0),
                q_of(g, cols),
                ROWS_ROWS,
                preferred_element_type=jnp.float32,
            )
            logits = logits * inv_root
            first = PLANE * BLOCKS
            pieces = [logits[:first] + biases[g][...]]
            for j in range(FIRST):
                pieces.append(logits[first + j * BLOCK : first + (j + 1) * BLOCK] + slot_rows[j])
            logits = jnp.concatenate(pieces, axis=0)
            top = jnp.max(logits, axis=0, keepdims=True)
            weights = jnp.exp(logits - top)
            tops[g][h : h + 1] = top
            sums[g][h : h + 1] = jnp.sum(weights, axis=0, keepdims=True)
            accs[g][cols] = lax.dot_general(
                jnp.concatenate(values, axis=0),
                weights.astype(jnp.bfloat16),
                COLS_COLS,
                preferred_element_type=jnp.float32,
            )

    for g in range(count):

        def chunk(ci, carry, g=g):
            first = FIRST + ci * CHUNK
            for j in range(CHUNK):
                arrived(g, first + j)
            slot_rows = [slot_bias(g, first + j) for j in range(CHUNK)]
            for h in range(heads):
                cols = pl.ds(h * HD, HD)
                keys = [bufs[g][first + j, :BLOCK, cols] for j in range(CHUNK)]
                values = [bufs[g][first + j, BLOCK:, cols] for j in range(CHUNK)]
                logits = lax.dot_general(
                    jnp.concatenate(keys, axis=0),
                    q_of(g, cols),
                    ROWS_ROWS,
                    preferred_element_type=jnp.float32,
                )
                logits = logits * inv_root
                pieces = [
                    logits[j * BLOCK : (j + 1) * BLOCK] + slot_rows[j] for j in range(CHUNK)
                ]
                logits = jnp.concatenate(pieces, axis=0)
                before = tops[g][h : h + 1]
                top = jnp.maximum(before, jnp.max(logits, axis=0, keepdims=True))
                weights = jnp.exp(logits - top)
                ratio = jnp.exp(before - top)
                tops[g][h : h + 1] = top
                sums[g][h : h + 1] = sums[g][h : h + 1] * ratio + jnp.sum(
                    weights, axis=0, keepdims=True
                )
                accs[g][cols] = accs[g][cols] * ratio + lax.dot_general(
                    jnp.concatenate(values, axis=0),
                    weights.astype(jnp.bfloat16),
                    COLS_COLS,
                    preferred_element_type=jnp.float32,
                )
            return carry

        lax.fori_loop(0, chunks[g], chunk, 0)

    for g in range(count):
        top = tops[g][...]
        sent = top.astype(jnp.bfloat16).astype(jnp.float32)
        factor = jnp.exp(top - sent)
        for h in range(heads):
            cols = pl.ds(h * HD, HD)
            out_refs[g][cols] = (accs[g][cols] * factor[h : h + 1]).astype(jnp.bfloat16)
        write_stats(out_refs[g], slice(None), heads, sent, sums[g][...] * factor)


def write_stats(out_ref, lanes, heads, top, total):
    high = total.astype(jnp.bfloat16).astype(jnp.float32)
    rows = (top, high, total - high, jnp.zeros_like(top))
    valid = iota(top.shape, 0) < heads
    rows = [jnp.where(valid, r, 0.0) for r in rows]
    out_ref[heads * HD :, lanes] = jnp.concatenate(rows, axis=0).astype(jnp.bfloat16)


def part(position, key_refs, value_refs, queries, groups):
    columns = queries[0].shape[1]
    heads = columns // HD
    wanted = FIRST + MOST
    vmem = pl.BlockSpec(memory_space=pltpu.VMEM)
    smem = pl.BlockSpec(memory_space=pltpu.SMEM)
    hbm = pl.BlockSpec(memory_space=pltpu.HBM)
    widths = [group[2] * BLOCK for group in groups]
    count = len(groups)
    scratch = [pltpu.VMEM((wanted, 2 * BLOCK, columns), jnp.bfloat16)] * count
    scratch += [pltpu.VMEM((columns, w), jnp.float32) for w in widths]
    scratch += [pltpu.VMEM((8, w), jnp.float32) for w in widths] * 2
    scratch += [pltpu.VMEM((PLANE * BLOCKS, w), jnp.float32) for w in widths]
    scratch += [
        pltpu.VMEM((PLANE, MEANS, columns), jnp.bfloat16),
        pltpu.VMEM((count, BLOCKS, HD), jnp.int32),
        pltpu.SMEM((count, BLOCKS, HD), jnp.int32),
    ]
    scratch += [pltpu.SMEM((count, wanted), jnp.int32)] * 2
    scratch += [pltpu.SemaphoreType.DMA((count, wanted))] * 2
    scratch += [pltpu.SemaphoreType.DMA((PLANE,)), pltpu.SemaphoreType.DMA((count,))]
    return pl.pallas_call(
        functools.partial(part_kernel, heads, groups),
        in_specs=[smem] + [vmem] * count + [hbm] * (2 * PLANE),
        out_specs=[vmem] * count,
        out_shape=[jax.ShapeDtypeStruct((columns + STATS, w), jnp.bfloat16) for w in widths],
        scratch_shapes=scratch,
        compiler_params=PARAMS,
        cost_estimate=pl.CostEstimate(
            flops=4 * 512 * 1024 * columns, bytes_accessed=4 * 1024 * 1024, transcendentals=500000
        ),
    )(position, *queries, *key_refs, *value_refs)


def stats_of(ref, lanes, heads):
    rows = ref[heads * HD :, lanes].astype(jnp.float32)
    return rows[:8], rows[8:16] + rows[16:24]


def merged(heads, parts):
    stats = [stats_of(ref, lanes, heads) for ref, lanes in parts]
    top = functools.reduce(jnp.maximum, [s[0] for s in stats])
    ratios = [jnp.exp(s[0] - top) for s in stats]
    total = functools.reduce(jnp.add, [r * s[1] for r, s in zip(ratios, stats)])
    return top, ratios, total


def merge_kernel(heads, up_ref, up_in_ref, down_ref, down_in_ref, up_out, down_out):
    for own, came, out, up in (
        (up_ref, up_in_ref, up_out, True),
        (down_ref, down_in_ref, down_out, False),
    ):
        width = came.shape[1]
        if width == own.shape[1]:
            lanes = slice(None)
        else:
            lanes = slice(0, width) if up else slice(width, 2 * width)
            rest = slice(width, 2 * width) if up else slice(0, width)
            out[:, rest] = own[:, rest]
        top, ratios, total = merged(heads, ((own, lanes), (came, slice(None))))
        for h in range(heads):
            cols = pl.ds(h * HD, HD)
            one = own[cols, lanes].astype(jnp.float32) * ratios[0][h : h + 1]
            two = came[cols, :].astype(jnp.float32) * ratios[1][h : h + 1]
            out[cols, lanes] = (one + two).astype(jnp.bfloat16)
        write_stats(out, lanes, heads, top, total)


def merge(up, up_in, down, down_in):
    heads = (up.shape[0] - STATS) // HD
    whole = jax.ShapeDtypeStruct(up.shape, jnp.bfloat16)
    return pl.pallas_call(
        functools.partial(merge_kernel, heads),
        out_shape=(whole, whole),
        compiler_params=PARAMS,
        cost_estimate=pl.CostEstimate(
            flops=1000000, bytes_accessed=2 * 1024 * 1024, transcendentals=1000
        ),
    )(up, up_in, down, down_in)


def last_kernel(heads, own_ref, up_ref, down_ref, out_ref):
    refs = (own_ref, up_ref, down_ref)
    _, ratios, total = merged(heads, [(ref, slice(None)) for ref in refs])
    valid = iota(total.shape, 0) < heads
    scales = [r / jnp.where(valid, total, 1.0) for r in ratios]
    for h in range(heads):
        cols = pl.ds(h * HD, HD)
        whole = jnp.zeros((HD, TOKENS), jnp.float32)
        for ref, scale in zip(refs, scales):
            whole = whole + ref[cols].astype(jnp.float32) * scale[h : h + 1]
        out_ref[:, cols] = jnp.transpose(whole).astype(out_ref.dtype)


def last(own, up, down):
    columns = own.shape[0] - STATS
    return pl.pallas_call(
        functools.partial(last_kernel, columns // HD),
        out_shape=jax.ShapeDtypeStruct((TOKENS, columns), jnp.bfloat16),
        compiler_params=PARAMS,
    )(own, up, down)


def body(queries, key_tokens, value_tokens, pair_keys, pair_count):
    tok_rows, columns = queries.shape
    assert lax.axis_size("ctx") == NX * NZ * NC
    assert tok_rows == TOKENS and pair_keys.shape == (BLOCKS, SLOTS)
    me = lax.axis_index("ctx")
    position = jnp.stack((me // (NZ * NC), (me // NC) % NZ, me % NC)).astype(jnp.int32)
    barrier = lax.optimization_barrier

    asked = jnp.concatenate(
        (pair_keys // BLOCKS, pair_keys % BLOCKS, pair_count[:, None]), axis=1
    ).astype(jnp.bfloat16)
    asked = jnp.pad(asked, ((0, REQUEST - BLOCKS), (0, columns - 2 * SLOTS - 1)))
    pay = jnp.concatenate((queries[:HALF], asked, queries[HALF:]), axis=0)

    def means(tokens):
        grouped = tokens.reshape(BLOCKS, BLOCK, columns).astype(jnp.float32)
        return jnp.mean(grouped, axis=1).astype(jnp.bfloat16)

    split = TOKENS + MEANS
    own = jnp.concatenate(
        (key_tokens, means(key_tokens), means(value_tokens), value_tokens), axis=0
    )
    pay, own = barrier((pay, own))
    up1, down1 = move(pay, dz=1), move(pay, dz=-1)
    left, right = move(own, dx=1), move(own, dx=-1)
    own_twin = move(own, dc=1)
    up1, down1, left, right, own_twin = barrier((up1, down1, left, right, own_twin))

    up2, down2 = move(up1, dz=1), move(down1, dz=-1)
    far_k, far_v = move(left[:split], dx=1), move(right[split:], dx=-1)
    left_twin = move(left, dc=1)
    up2, down2, far_k, far_v, left_twin = barrier((up2, down2, far_k, far_v, left_twin))

    up3, down3 = move(up2, dz=1), move(down2, dz=-1)
    right_twin, far_k_twin, far_v_twin = move(right, dc=1), move(far_k, dc=1), move(far_v, dc=1)
    up3, down3, right_twin, far_k_twin, far_v_twin = barrier(
        (up3, down3, right_twin, far_k_twin, far_v_twin)
    )
    far_up = move(up3[: HALF + REQUEST], dz=1)
    far_down = move(down3[HALF:], dz=-1)

    key_refs = (own, own_twin, right, right_twin, far_k, far_k_twin, left, left_twin)
    value_refs = (own, own_twin, right, right_twin, far_v, far_v_twin, left, left_twin)
    attend = functools.partial(part, position, key_refs, value_refs)
    both, last_half = (0, HALF + REQUEST), BLOCKS // 2

    up_in, down_in = attend(
        (far_up, far_down), (((0,), 0, last_half, HALF), ((REQUEST,), last_half, last_half, 0))
    )
    up_in, down_in = move(up_in, dz=-1), move(down_in, dz=1)
    for up, down in ((up3, down3), (up2, down2), (up1, down1)):
        up_part, down_part = attend((up, down), ((both, 0, BLOCKS, HALF),) * 2)
        up_sum, down_sum = merge(up_part, up_in, down_part, down_in)
        up_in, down_in = move(up_sum, dz=-1), move(down_sum, dz=1)
    (own_part,) = attend((pay,), ((both, 0, BLOCKS, HALF),))
    return last(own_part, up_in, down_in)


def solution(mesh):
    placed = (P("ctx", "head"), P("ctx", "head"), P("ctx", "head"), P("ctx", None), P("ctx"))
    return jax.shard_map(
        body, mesh=mesh, in_specs=placed, out_specs=P("ctx", "head"), check_vma=False
    )
```

profile of v0, /device:TPU:8, one launch (start us, length us, event | category | flops | bytes accessed | tf_op | source)
XLA Modules:
  0.0 117.8 jit_solution(10600966023175986415)
XLA Ops:
  0.0 1.1 fusion.13
  1.1 0.7 convert_bitcast_fusion
  1.8 0.1 copy.10
  1.9 0.8 copy.6
  2.6 0.1 convert_reduce_fusion
  2.7 0.1 convert_reduce_fusion.1
  2.9 0.1 fusion.8
  3.0 1.6 %collective-permute-start.2 = (bf16[528,640]{1,0:T(8,128)(2,1)S(1)}, bf16[528,640]{1,0:T(8,128)(2,1)S(1)}, u32[]{:S(2)}, u32[]{:S(2)}) collective-permute-start(bf16[528,640]{1,0:T(8,128)(2,1)S(1)} %pad_maximum_fusion.rest_1_.rest_9_.rest_2_.rest_10_), channel_id=1, source_target_pairs={{0,64},{4,68},{8,72},{12,76},{16,80},{20,84},{24,88},{28,92},{32,9... | collective-permute-start | bytes 2027528 | tf_op jit(solution)/shard_map/ppermute | solution.py:38
  4.6 1.7 %collective-permute-start.3 = (bf16[528,640]{1,0:T(8,128)(2,1)S(1)}, bf16[528,640]{1,0:T(8,128)(2,1)S(1)}, u32[]{:S(2)}, u32[]{:S(2)}) collective-permute-start(bf16[528,640]{1,0:T(8,128)(2,1)S(1)} %pad_maximum_fusion.rest_1_.rest_9_.rest_2_.rest_10_), channel_id=1, source_target_pairs={{0,192},{4,196},{8,200},{12,204},{16,208},{20,212},{24,216},{28,22... | collective-permute-start | bytes 2027528 | tf_op jit(solution)/shard_map/ppermute | solution.py:38
  6.3 1.9 %collective-permute-start = (bf16[272,640]{1,0:T(8,128)(2,1)S(1)}, bf16[272,640]{1,0:T(8,128)(2,1)S(1)}, u32[]{:S(2)}, u32[]{:S(2)}) collective-permute-start(bf16[272,640]{1,0:T(8,128)(2,1)S(1)} %pad_maximum_fusion.1.rest_0_), channel_id=1, source_target_pairs={{0,8},{4,12},{8,16},{12,20},{16,24},{20,28},{24,32},{28,36},{32,40... | collective-permute-start | bytes 1044488 | tf_op jit(solution)/shard_map/ppermute | solution.py:38
  8.2 3.9 %collective-permute-start.1 = (bf16[272,640]{1,0:T(8,128)(2,1)S(1)}, bf16[272,640]{1,0:T(8,128)(2,1)S(1)}, u32[]{:S(2)}, u32[]{:S(2)}) collective-permute-start(bf16[272,640]{1,0:T(8,128)(2,1)S(1)} %pad_maximum_fusion.1.rest_0_), channel_id=1, source_target_pairs={{0,56},{4,60},{8,0},{12,4},{16,8},{20,12},{24,16},{28,20},{32,24},... | collective-permute-start | bytes 1044488 | tf_op jit(solution)/shard_map/ppermute | solution.py:38
  12.2 0.7 copy-done.12
  12.9 8.1 %collective-permute-done.rest_0_ = bf16[272,640]{1,0:T(8,128)(2,1)S(1)} collective-permute-done((bf16[272,640]{1,0:T(8,128)(2,1)S(1)}, bf16[272,640]{1,0:T(8,128)(2,1)S(1)}, u32[]{:S(2)}, u32[]{:S(2)}) %collective-permute-start) | collective-permute-done | bytes 348192 | tf_op jit(solution)/shard_map/ppermute | solution.py:38
  21.0 0.2 collective-permute-done.2.rest_7_.rest_15_.rest_8_.rest_16_
  21.3 3.0 %collective-permute-start.8 = (bf16[256,640]{1,0:T(8,128)(2,1)S(1)}, bf16[256,640]{1,0:T(8,128)(2,1)S(1)}, u32[]{:S(2)}, u32[]{:S(2)}) collective-permute-start(bf16[256,640]{1,0:T(8,128)(2,1)S(1)} %slice.21), channel_id=1, source_target_pairs={{0,192},{4,196},{8,200},{12,204},{16,208},{20,212},{24,216},{28,22... | collective-permute-start | bytes 983048 | tf_op jit(solution)/shard_map/ppermute | solution.py:38
  24.3 2.0 %collective-permute-start.5 = (bf16[272,640]{1,0:T(8,128)(2,1)S(1)}, bf16[272,640]{1,0:T(8,128)(2,1)S(1)}, u32[]{:S(2)}, u32[]{:S(2)}) collective-permute-start(bf16[272,640]{1,0:T(8,128)(2,1)S(1)} %collective-permute-done.rest_0_), channel_id=1, source_target_pairs={{0,8},{4,12},{8,16},{12,20},{16,24},{20,28},{24,32},{28,36},{32,40... | collective-permute-start | bytes 1044488 | tf_op jit(solution)/shard_map/ppermute | solution.py:38
  26.3 4.0 %collective-permute-start.6 = (bf16[272,640]{1,0:T(8,128)(2,1)S(1)}, bf16[272,640]{1,0:T(8,128)(2,1)S(1)}, u32[]{:S(2)}, u32[]{:S(2)}) collective-permute-start(bf16[272,640]{1,0:T(8,128)(2,1)S(1)} %collective-permute-done.1.rest_1_), channel_id=1, source_target_pairs={{0,56},{4,60},{8,0},{12,4},{16,8},{20,12},{24,16},{28,20},{32,24},... | collective-permute-start | bytes 1044488 | tf_op jit(solution)/shard_map/ppermute | solution.py:38
  30.4 1.6 %collective-permute-done.8.rest_13_.rest_14_ = bf16[256,640]{1,0:T(8,128)(2,1)S(1)} collective-permute-done((bf16[256,640]{1,0:T(8,128)(2,1)S(1)}, bf16[256,640]{1,0:T(8,128)(2,1)S(1)}, u32[]{:S(2)}, u32[]{:S(2)}) %collective-permute-start.8) | collective-permute-done | bytes 327712 | tf_op jit(solution)/shard_map/ppermute | solution.py:38
  31.9 6.9 %collective-permute-done.5.rest_0_ = bf16[272,640]{1,0:T(8,128)(2,1)S(1)} collective-permute-done((bf16[272,640]{1,0:T(8,128)(2,1)S(1)}, bf16[272,640]{1,0:T(8,128)(2,1)S(1)}, u32[]{:S(2)}, u32[]{:S(2)}) %collective-permute-start.5) | collective-permute-done | bytes 348192 | tf_op jit(solution)/shard_map/ppermute | solution.py:38
  38.8 2.8 %collective-permute-done.7.rest_5_.rest_6_ = bf16[272,640]{1,0:T(8,128)(2,1)S(1)} collective-permute-done((bf16[272,640]{1,0:T(8,128)(2,1)S(1)}, bf16[272,640]{1,0:T(8,128)(2,1)S(1)}, u32[]{:S(2)}, u32[]{:S(2)}) %collective-permute-start.7) | collective-permute-done | bytes 348192 | tf_op jit(solution)/shard_map/ppermute | solution.py:38
  41.6 0.7 copy-done.22
  42.3 3.2 %collective-permute-start.11 = (bf16[272,640]{1,0:T(8,128)(2,1)S(1)}, bf16[272,640]{1,0:T(8,128)(2,1)S(1)}, u32[]{:S(2)}, u32[]{:S(2)}) collective-permute-start(bf16[272,640]{1,0:T(8,128)(2,1)S(1)} %collective-permute-done.6.rest_1_), channel_id=1, source_target_pairs={{0,56},{4,60},{8,0},{12,4},{16,8},{20,12},{24,16},{28,20},{32,24},... | collective-permute-start | bytes 1044488 | tf_op jit(solution)/shard_map/ppermute | solution.py:38
  45.6 0.8 copy-done.24
  46.3 0.7 copy-done.3
  47.1 0.5 collective-permute-start.14
  47.6 0.7 copy-done.8
  48.3 0.9 copy-done
  49.2 0.7 copy-done.10
  49.9 2.0 %collective-permute-done.10.rest_0_ = bf16[272,640]{1,0:T(8,128)(2,1)S(1)} collective-permute-done((bf16[272,640]{1,0:T(8,128)(2,1)S(1)}, bf16[272,640]{1,0:T(8,128)(2,1)S(1)}, u32[]{:S(2)}, u32[]{:S(2)}) %collective-permute-start.10) | collective-permute-done | bytes 348192 | tf_op jit(solution)/shard_map/ppermute | solution.py:38
  52.0 0.7 copy-done.5
  52.7 0.7 slice.22
  53.4 0.7 copy-done.14
  54.1 0.4 collective-permute-start.15
  54.5 0.7 slice.23
  55.3 0.8 copy-done.16
  56.0 3.3 %collective-permute-start.16 = (bf16[144,640]{1,0:T(8,128)(2,1)}, bf16[144,640]{1,0:T(8,128)(2,1)}, u32[]{:S(2)}, u32[]{:S(2)}) collective-permute-start(bf16[144,640]{1,0:T(8,128)(2,1)} %slice.23), channel_id=1, source_target_pairs={{0,56},{4,60},{8,0},{12,4},{16,8},{20,12},{24,16},{28,20},{32,24},... | collective-permute-start | bytes 552968 | tf_op jit(solution)/shard_map/ppermute | solution.py:38
  59.3 2.3 %collective-permute-done.15.rest_0_ = bf16[144,640]{1,0:T(8,128)(2,1)} collective-permute-done((bf16[144,640]{1,0:T(8,128)(2,1)}, bf16[144,640]{1,0:T(8,128)(2,1)}, u32[]{:S(2)}, u32[]{:S(2)}) %collective-permute-start.15) | collective-permute-done | bytes 184352 | tf_op jit(solution)/shard_map/ppermute | solution.py:38
  61.6 1.0 collective-permute-done.16.rest_1_
  62.6 1.1 copy-done.1
  63.7 1.0 copy-done.4
  64.7 1.0 copy-done.6
  65.7 1.0 copy-done.9
  66.7 1.0 copy-done.11
  67.6 5.7 %shard_map.59 = (bf16[672,128]{1,0:T(8,128)(2,1)S(1)}, bf16[672,128]{1,0:T(8,128)(2,1)S(1)}) custom-call(s32[3]{0:T(128)S(1)} %pad_add_fusion.pos_ref, bf16[144,640]{1,0:T(8,128)(2,1)} %collective-permute-done.15.rest_0_, bf16[144,640]{1,0:T(8,128)(2,1)} %collective-permute-done.16.rest_1_, ...), custom_call_target="tpu_custom_call" | custom-call | flops 1342177280 | bytes 4194304 | tf_op jit(solution)/shard_map/pallas_call | solution.py:271
  73.4 3.8 %collective-permute-start.17 = (bf16[672,128]{1,0:T(8,128)(2,1)S(1)}, bf16[672,128]{1,0:T(8,128)(2,1)S(1)}, u32[]{:S(2)}, u32[]{:S(2)}) collective-permute-start(bf16[672,128]{1,0:T(8,128)(2,1)S(1)} %get-tuple-element.56), channel_id=1, source_target_pairs={{0,56},{4,60},{8,0},{12,4},{16,8},{20,12},{24,16},{28,20},{32,24},... | collective-permute-start | bytes 516104 | tf_op jit(solution)/shard_map/ppermute | solution.py:38
  77.2 4.7 %shard_map.58 = (bf16[672,256]{1,0:T(8,128)(2,1)S(1)}, bf16[672,256]{1,0:T(8,128)(2,1)S(1)}) custom-call(s32[3]{0:T(128)S(1)} %pad_add_fusion.pos_ref, bf16[272,640]{1,0:T(8,128)(2,1)S(1)} %copy-done.15, bf16[272,640]{1,0:T(8,128)(2,1)S(1)} %copy-done.17, bf16[528,640]{1,0:T(8,128)(2,1)S(1)} %pad_maximum_fusion.rest_1_.rest_9_.rest_2_.rest_10_, ...), custom_call_target="tpu_custom_call" | custom-call | flops 1342177280 | bytes 4194304 | tf_op jit(solution)/shard_map/pallas_call | solution.py:271
  81.9 1.9 %collective-permute-done.18.down_in_ref = bf16[672,128]{1,0:T(8,128)(2,1)S(1)} collective-permute-done((bf16[672,128]{1,0:T(8,128)(2,1)S(1)}, bf16[672,128]{1,0:T(8,128)(2,1)S(1)}, u32[]{:S(2)}, u32[]{:S(2)}) %collective-permute-start.18) | collective-permute-done | bytes 172064 | tf_op jit(solution)/shard_map/ppermute | solution.py:38
  83.8 0.2 shard_map.60
  84.0 2.5 %collective-permute-start.19 = (bf16[672,256]{1,0:T(8,128)(2,1)S(1)}, bf16[672,256]{1,0:T(8,128)(2,1)S(1)}, u32[]{:S(2)}, u32[]{:S(2)}) collective-permute-start(bf16[672,256]{1,0:T(8,128)(2,1)S(1)} %get-tuple-element.59), channel_id=1, source_target_pairs={{0,56},{4,60},{8,0},{12,4},{16,8},{20,12},{24,16},{28,20},{32,24},... | collective-permute-start | bytes 1032200 | tf_op jit(solution)/shard_map/ppermute | solution.py:38
  86.5 6.0 %shard_map.57 = (bf16[672,256]{1,0:T(8,128)(2,1)S(1)}, bf16[672,256]{1,0:T(8,128)(2,1)S(1)}) custom-call(s32[3]{0:T(128)S(1)} %pad_add_fusion.pos_ref, bf16[272,640]{1,0:T(8,128)(2,1)S(1)} %copy-done.23, bf16[272,640]{1,0:T(8,128)(2,1)S(1)} %copy-done.25, bf16[528,640]{1,0:T(8,128)(2,1)S(1)} %pad_maximum_fusion.rest_1_.rest_9_.rest_2_.rest_10_, ...), custom_call_target="tpu_custom_call" | custom-call | flops 1342177280 | bytes 4194304 | tf_op jit(solution)/shard_map/pallas_call | solution.py:271
  92.5 3.9 %collective-permute-done.20.down_in_ref = bf16[672,256]{1,0:T(8,128)(2,1)S(1)} collective-permute-done((bf16[672,256]{1,0:T(8,128)(2,1)S(1)}, bf16[672,256]{1,0:T(8,128)(2,1)S(1)}, u32[]{:S(2)}, u32[]{:S(2)}) %collective-permute-start.20) | collective-permute-done | bytes 344096 | tf_op jit(solution)/shard_map/ppermute | solution.py:38
  96.4 0.3 shard_map.61
  96.6 0.1 collective-permute-start.21
  96.7 2.0 %collective-permute-start.22 = (bf16[672,256]{1,0:T(8,128)(2,1)S(1)}, bf16[672,256]{1,0:T(8,128)(2,1)S(1)}, u32[]{:S(2)}, u32[]{:S(2)}) collective-permute-start(bf16[672,256]{1,0:T(8,128)(2,1)S(1)} %get-tuple-element.64), channel_id=1, source_target_pairs={{0,8},{4,12},{8,16},{12,20},{16,24},{20,28},{24,32},{28,36},{32,40... | collective-permute-start | bytes 1032200 | tf_op jit(solution)/shard_map/ppermute | solution.py:38
  98.7 6.8 %shard_map.56 = (bf16[672,256]{1,0:T(8,128)(2,1)S(1)}, bf16[672,256]{1,0:T(8,128)(2,1)S(1)}) custom-call(s32[3]{0:T(128)S(1)} %pad_add_fusion.pos_ref, bf16[272,640]{1,0:T(8,128)(2,1)S(1)} %copy-done.19, bf16[272,640]{1,0:T(8,128)(2,1)S(1)} %copy-done.21, bf16[528,640]{1,0:T(8,128)(2,1)S(1)} %pad_maximum_fusion.rest_1_.rest_9_.rest_2_.rest_10_, ...), custom_call_target="tpu_custom_call" | custom-call | flops 1342177280 | bytes 4194304 | tf_op jit(solution)/shard_map/pallas_call | solution.py:271
  105.5 1.0 collective-permute-done.21.up_in_ref
  106.5 1.3 %collective-permute-done.22.down_in_ref = bf16[672,256]{1,0:T(8,128)(2,1)S(1)} collective-permute-done((bf16[672,256]{1,0:T(8,128)(2,1)S(1)}, bf16[672,256]{1,0:T(8,128)(2,1)S(1)}, u32[]{:S(2)}, u32[]{:S(2)}) %collective-permute-start.22) | collective-permute-done | bytes 344096 | tf_op jit(solution)/shard_map/ppermute | solution.py:38
  107.8 0.3 shard_map.62
  108.1 0.1 collective-permute-start.23
  108.2 2.0 %collective-permute-start.24 = (bf16[672,256]{1,0:T(8,128)(2,1)S(1)}, bf16[672,256]{1,0:T(8,128)(2,1)S(1)}, u32[]{:S(2)}, u32[]{:S(2)}) collective-permute-start(bf16[672,256]{1,0:T(8,128)(2,1)S(1)} %get-tuple-element.66), channel_id=1, source_target_pairs={{0,8},{4,12},{8,16},{12,20},{16,24},{20,28},{24,32},{28,36},{32,40... | collective-permute-start | bytes 1032200 | tf_op jit(solution)/shard_map/ppermute | solution.py:38
  110.2 2.9 %shard_map.55.own_ref = bf16[672,256]{1,0:T(8,128)(2,1)S(1)} custom-call(s32[3]{0:T(128)S(1)} %pad_add_fusion.pos_ref, bf16[272,640]{1,0:T(8,128)(2,1)S(1)} %copy-done.13, bf16[528,640]{1,0:T(8,128)(2,1)S(1)} %pad_maximum_fusion.rest_1_.rest_9_.rest_2_.rest_10_, bf16[528,640]{1,0:T(8,128)(2,1)S(1)} %collective-permute-done.4.rest_2_.rest_10_.rest_3_.rest_11_, ...), custom_call_target="tpu_custom_call" | custom-call | flops 1342177280 | bytes 4194304 | tf_op jit(solution)/shard_map/pallas_call | solution.py:271
  113.1 2.3 %collective-permute-done.23.up_ref = bf16[672,256]{1,0:T(8,128)(2,1)S(1)} collective-permute-done((bf16[672,256]{1,0:T(8,128)(2,1)S(1)}, bf16[672,256]{1,0:T(8,128)(2,1)S(1)}, u32[]{:S(2)}, u32[]{:S(2)}) %collective-permute-start.23) | collective-permute-done | bytes 344096 | tf_op jit(solution)/shard_map/ppermute | solution.py:38
  115.5 1.3 %collective-permute-done.24.down_ref = bf16[672,256]{1,0:T(8,128)(2,1)S(1)} collective-permute-done((bf16[672,256]{1,0:T(8,128)(2,1)S(1)}, bf16[672,256]{1,0:T(8,128)(2,1)S(1)}, u32[]{:S(2)}, u32[]{:S(2)}) %collective-permute-start.24) | collective-permute-done | bytes 344096 | tf_op jit(solution)/shard_map/ppermute | solution.py:38
  116.8 1.0 shard_map.63
  (67 shorter events, 0.4 us)
Async XLA Ops:
  0.0 2.6 %copy-start.26 = (bf16[256,640]{1,0:T(8,128)(2,1)S(1)}, bf16[256,640]{1,0:T(8,128)(2,1)}, u32[]{:S(2)}) copy-start(bf16[256,640]{1,0:T(8,128)(2,1)} %param.7) | copy-start | bytes 983044
  0.0 2.7 %copy-start.27 = (bf16[256,640]{1,0:T(8,128)(2,1)S(1)}, bf16[256,640]{1,0:T(8,128)(2,1)}, u32[]{:S(2)}) copy-start(bf16[256,640]{1,0:T(8,128)(2,1)} %param.6) | copy-start | bytes 983044
  3.0 18.2 %collective-permute-start.2 = (bf16[528,640]{1,0:T(8,128)(2,1)S(1)}, bf16[528,640]{1,0:T(8,128)(2,1)S(1)}, u32[]{:S(2)}, u32[]{:S(2)}) collective-permute-start(bf16[528,640]{1,0:T(8,128)(2,1)S(1)} %pad_maximum_fusion.rest_1_.rest_9_.rest_2_.rest_10_), channel_id=1, source_target_pairs={{0,64},{4,68},{8,72},{12,76},{16,80},{20,84},{24,88},{28,92},{32,9... | collective-permute-start | bytes 2027528 | tf_op jit(solution)/shard_map/ppermute | solution.py:38
  4.6 16.6 %collective-permute-start.3 = (bf16[528,640]{1,0:T(8,128)(2,1)S(1)}, bf16[528,640]{1,0:T(8,128)(2,1)S(1)}, u32[]{:S(2)}, u32[]{:S(2)}) collective-permute-start(bf16[528,640]{1,0:T(8,128)(2,1)S(1)} %pad_maximum_fusion.rest_1_.rest_9_.rest_2_.rest_10_), channel_id=1, source_target_pairs={{0,192},{4,196},{8,200},{12,204},{16,208},{20,212},{24,216},{28,22... | collective-permute-start | bytes 2027528 | tf_op jit(solution)/shard_map/ppermute | solution.py:38
  6.3 14.9 %collective-permute-start.4 = (bf16[528,640]{1,0:T(8,128)(2,1)S(1)}, bf16[528,640]{1,0:T(8,128)(2,1)S(1)}, u32[]{:S(2)}, u32[]{:S(2)}) collective-permute-start(bf16[528,640]{1,0:T(8,128)(2,1)S(1)} %pad_maximum_fusion.rest_1_.rest_9_.rest_2_.rest_10_), channel_id=1, source_target_pairs={{0,4},{4,0},{8,12},{12,8},{16,20},{20,16},{24,28},{28,24},{32,36},... | collective-permute-start | bytes 2027528 | tf_op jit(solution)/shard_map/ppermute | solution.py:38
  6.3 14.7 %collective-permute-start = (bf16[272,640]{1,0:T(8,128)(2,1)S(1)}, bf16[272,640]{1,0:T(8,128)(2,1)S(1)}, u32[]{:S(2)}, u32[]{:S(2)}) collective-permute-start(bf16[272,640]{1,0:T(8,128)(2,1)S(1)} %pad_maximum_fusion.1.rest_0_), channel_id=1, source_target_pairs={{0,8},{4,12},{8,16},{12,20},{16,24},{20,28},{24,32},{28,36},{32,40... | collective-permute-start | bytes 1044488 | tf_op jit(solution)/shard_map/ppermute | solution.py:38
  8.2 12.8 %collective-permute-start.1 = (bf16[272,640]{1,0:T(8,128)(2,1)S(1)}, bf16[272,640]{1,0:T(8,128)(2,1)S(1)}, u32[]{:S(2)}, u32[]{:S(2)}) collective-permute-start(bf16[272,640]{1,0:T(8,128)(2,1)S(1)} %pad_maximum_fusion.1.rest_0_), channel_id=1, source_target_pairs={{0,56},{4,60},{8,0},{12,4},{16,8},{20,12},{24,16},{28,20},{32,24},... | collective-permute-start | bytes 1044488 | tf_op jit(solution)/shard_map/ppermute | solution.py:38
  12.2 0.7 copy-start.12
  21.0 3.3 %copy-start.18 = (bf16[272,640]{1,0:T(8,128)(2,1)}, bf16[272,640]{1,0:T(8,128)(2,1)S(1)}, u32[]{:S(2)}) copy-start(bf16[272,640]{1,0:T(8,128)(2,1)S(1)} %collective-permute-done.rest_0_) | copy-start | bytes 1044484
  21.0 5.3 %copy-start.20 = (bf16[272,640]{1,0:T(8,128)(2,1)}, bf16[272,640]{1,0:T(8,128)(2,1)S(1)}, u32[]{:S(2)}) copy-start(bf16[272,640]{1,0:T(8,128)(2,1)S(1)} %collective-permute-done.1.rest_1_) | copy-start | bytes 1044484
  21.2 20.4 %collective-permute-start.9 = (bf16[528,640]{1,0:T(8,128)(2,1)S(1)}, bf16[528,640]{1,0:T(8,128)(2,1)S(1)}, u32[]{:S(2)}, u32[]{:S(2)}) collective-permute-start(bf16[528,640]{1,0:T(8,128)(2,1)S(1)} %collective-permute-done.2.rest_7_.rest_15_.rest_8_.rest_16_), channel_id=1, source_target_pairs={{0,4},{4,0},{8,12},{12,8},{16,20},{20,16},{24,28},{28,24},{32,36},... | collective-permute-start | bytes 2027528 | tf_op jit(solution)/shard_map/ppermute | solution.py:38
  21.3 10.7 %collective-permute-start.8 = (bf16[256,640]{1,0:T(8,128)(2,1)S(1)}, bf16[256,640]{1,0:T(8,128)(2,1)S(1)}, u32[]{:S(2)}, u32[]{:S(2)}) collective-permute-start(bf16[256,640]{1,0:T(8,128)(2,1)S(1)} %slice.21), channel_id=1, source_target_pairs={{0,192},{4,196},{8,200},{12,204},{16,208},{20,212},{24,216},{28,22... | collective-permute-start | bytes 983048 | tf_op jit(solution)/shard_map/ppermute | solution.py:38
  24.3 14.5 %collective-permute-start.5 = (bf16[272,640]{1,0:T(8,128)(2,1)S(1)}, bf16[272,640]{1,0:T(8,128)(2,1)S(1)}, u32[]{:S(2)}, u32[]{:S(2)}) collective-permute-start(bf16[272,640]{1,0:T(8,128)(2,1)S(1)} %collective-permute-done.rest_0_), channel_id=1, source_target_pairs={{0,8},{4,12},{8,16},{12,20},{16,24},{20,28},{24,32},{28,36},{32,40... | collective-permute-start | bytes 1044488 | tf_op jit(solution)/shard_map/ppermute | solution.py:38
  26.3 12.5 %collective-permute-start.6 = (bf16[272,640]{1,0:T(8,128)(2,1)S(1)}, bf16[272,640]{1,0:T(8,128)(2,1)S(1)}, u32[]{:S(2)}, u32[]{:S(2)}) collective-permute-start(bf16[272,640]{1,0:T(8,128)(2,1)S(1)} %collective-permute-done.1.rest_1_), channel_id=1, source_target_pairs={{0,56},{4,60},{8,0},{12,4},{16,8},{20,12},{24,16},{28,20},{32,24},... | collective-permute-start | bytes 1044488 | tf_op jit(solution)/shard_map/ppermute | solution.py:38
  30.4 11.2 %collective-permute-start.7 = (bf16[272,640]{1,0:T(8,128)(2,1)S(1)}, bf16[272,640]{1,0:T(8,128)(2,1)S(1)}, u32[]{:S(2)}, u32[]{:S(2)}) collective-permute-start(bf16[272,640]{1,0:T(8,128)(2,1)S(1)} %slice.20), channel_id=1, source_target_pairs={{0,64},{4,68},{8,72},{12,76},{16,80},{20,84},{24,88},{28,92},{32,9... | collective-permute-start | bytes 1044488 | tf_op jit(solution)/shard_map/ppermute | solution.py:38
  31.9 16.4 %collective-permute-start.12 = (bf16[528,640]{1,0:T(8,128)(2,1)S(1)}, bf16[528,640]{1,0:T(8,128)(2,1)S(1)}, u32[]{:S(2)}, u32[]{:S(2)}) collective-permute-start(bf16[528,640]{1,0:T(8,128)(2,1)S(1)} %collective-permute-done.3.rest_3_.rest_11_.rest_4_.rest_12_), channel_id=1, source_target_pairs={{0,4},{4,0},{8,12},{12,8},{16,20},{20,16},{24,28},{28,24},{32,36},... | collective-permute-start | bytes 2027528 | tf_op jit(solution)/shard_map/ppermute | solution.py:38
  41.6 10.4 %collective-permute-start.10 = (bf16[272,640]{1,0:T(8,128)(2,1)S(1)}, bf16[272,640]{1,0:T(8,128)(2,1)S(1)}, u32[]{:S(2)}, u32[]{:S(2)}) collective-permute-start(bf16[272,640]{1,0:T(8,128)(2,1)S(1)} %collective-permute-done.5.rest_0_), channel_id=1, source_target_pairs={{0,8},{4,12},{8,16},{12,20},{16,24},{20,28},{24,32},{28,36},{32,40... | collective-permute-start | bytes 1044488 | tf_op jit(solution)/shard_map/ppermute | solution.py:38
  41.6 0.8 copy-start.22
  42.3 9.6 %collective-permute-start.11 = (bf16[272,640]{1,0:T(8,128)(2,1)S(1)}, bf16[272,640]{1,0:T(8,128)(2,1)S(1)}, u32[]{:S(2)}, u32[]{:S(2)}) collective-permute-start(bf16[272,640]{1,0:T(8,128)(2,1)S(1)} %collective-permute-done.6.rest_1_), channel_id=1, source_target_pairs={{0,56},{4,60},{8,0},{12,4},{16,8},{20,12},{24,16},{28,20},{32,24},... | collective-permute-start | bytes 1044488 | tf_op jit(solution)/shard_map/ppermute | solution.py:38
  45.6 0.8 copy-start.24
  46.3 5.6 %collective-permute-start.13 = (bf16[272,640]{1,0:T(8,128)(2,1)S(1)}, bf16[272,640]{1,0:T(8,128)(2,1)S(1)}, u32[]{:S(2)}, u32[]{:S(2)}) collective-permute-start(bf16[272,640]{1,0:T(8,128)(2,1)S(1)} %collective-permute-done.7.rest_5_.rest_6_), channel_id=1, source_target_pairs={{0,4},{4,0},{8,12},{12,8},{16,20},{20,16},{24,28},{28,24},{32,36},... | collective-permute-start | bytes 1044488 | tf_op jit(solution)/shard_map/ppermute | solution.py:38
  46.3 0.7 copy-start.3
  47.1 2.1 %collective-permute-start.14 = (bf16[256,640]{1,0:T(8,128)(2,1)S(1)}, bf16[256,640]{1,0:T(8,128)(2,1)S(1)}, u32[]{:S(2)}, u32[]{:S(2)}) collective-permute-start(bf16[256,640]{1,0:T(8,128)(2,1)S(1)} %collective-permute-done.8.rest_13_.rest_14_), channel_id=1, source_target_pairs={{0,4},{4,0},{8,12},{12,8},{16,20},{20,16},{24,28},{28,24},{32,36},... | collective-permute-start | bytes 983048 | tf_op jit(solution)/shard_map/ppermute | solution.py:38
  47.6 0.7 copy-start.8
  48.3 0.9 copy-start
  49.2 0.7 copy-start.10
  52.0 0.7 copy-start.5
  53.4 0.7 copy-start.14
  54.1 7.5 %collective-permute-start.15 = (bf16[144,640]{1,0:T(8,128)(2,1)}, bf16[144,640]{1,0:T(8,128)(2,1)}, u32[]{:S(2)}, u32[]{:S(2)}) collective-permute-start(bf16[144,640]{1,0:T(8,128)(2,1)} %slice.22), channel_id=1, source_target_pairs={{0,8},{4,12},{8,16},{12,20},{16,24},{20,28},{24,32},{28,36},{32,40... | collective-permute-start | bytes 552968 | tf_op jit(solution)/shard_map/ppermute | solution.py:38
  55.3 0.8 copy-start.16
  56.0 6.6 %collective-permute-start.16 = (bf16[144,640]{1,0:T(8,128)(2,1)}, bf16[144,640]{1,0:T(8,128)(2,1)}, u32[]{:S(2)}, u32[]{:S(2)}) collective-permute-start(bf16[144,640]{1,0:T(8,128)(2,1)} %slice.23), channel_id=1, source_target_pairs={{0,56},{4,60},{8,0},{12,4},{16,8},{20,12},{24,16},{28,20},{32,24},... | collective-permute-start | bytes 552968 | tf_op jit(solution)/shard_map/ppermute | solution.py:38
  62.6 1.1 copy-start.1
  63.7 1.0 copy-start.4
  64.7 1.0 copy-start.6
  65.7 1.0 copy-start.9
  66.7 1.0 copy-start.11
  67.6 9.5 %copy-start.15 = (bf16[272,640]{1,0:T(8,128)(2,1)S(1)}, bf16[272,640]{1,0:T(8,128)(2,1)}, u32[]{:S(2)}) copy-start(bf16[272,640]{1,0:T(8,128)(2,1)} %copy-done.14) | copy-start | bytes 1044484
  67.6 9.5 %copy-start.17 = (bf16[272,640]{1,0:T(8,128)(2,1)S(1)}, bf16[272,640]{1,0:T(8,128)(2,1)}, u32[]{:S(2)}) copy-start(bf16[272,640]{1,0:T(8,128)(2,1)} %copy-done.16) | copy-start | bytes 1044484
  73.4 8.5 %collective-permute-start.17 = (bf16[672,128]{1,0:T(8,128)(2,1)S(1)}, bf16[672,128]{1,0:T(8,128)(2,1)S(1)}, u32[]{:S(2)}, u32[]{:S(2)}) collective-permute-start(bf16[672,128]{1,0:T(8,128)(2,1)S(1)} %get-tuple-element.56), channel_id=1, source_target_pairs={{0,56},{4,60},{8,0},{12,4},{16,8},{20,12},{24,16},{28,20},{32,24},... | collective-permute-start | bytes 516104 | tf_op jit(solution)/shard_map/ppermute | solution.py:38
  77.1 6.6 %collective-permute-start.18 = (bf16[672,128]{1,0:T(8,128)(2,1)S(1)}, bf16[672,128]{1,0:T(8,128)(2,1)S(1)}, u32[]{:S(2)}, u32[]{:S(2)}) collective-permute-start(bf16[672,128]{1,0:T(8,128)(2,1)S(1)} %get-tuple-element.58), channel_id=1, source_target_pairs={{0,8},{4,12},{8,16},{12,20},{16,24},{20,28},{24,32},{28,36},{32,40... | collective-permute-start | bytes 516104 | tf_op jit(solution)/shard_map/ppermute | solution.py:38
  77.2 9.3 %copy-start.25 = (bf16[272,640]{1,0:T(8,128)(2,1)S(1)}, bf16[272,640]{1,0:T(8,128)(2,1)}, u32[]{:S(2)}) copy-start(bf16[272,640]{1,0:T(8,128)(2,1)} %copy-done.24) | copy-start | bytes 1044484
  81.8 4.6 %copy-start.7 = (bf16[272,640]{1,0:T(8,128)(2,1)S(1)}, bf16[272,640]{1,0:T(8,128)(2,1)}, u32[]{:S(2)}) copy-start(bf16[272,640]{1,0:T(8,128)(2,1)} %copy-done.5) | copy-start | bytes 1044484
  81.9 4.6 %copy-start.23 = (bf16[272,640]{1,0:T(8,128)(2,1)S(1)}, bf16[272,640]{1,0:T(8,128)(2,1)}, u32[]{:S(2)}) copy-start(bf16[272,640]{1,0:T(8,128)(2,1)} %copy-done.22) | copy-start | bytes 1044484
  84.0 8.5 %collective-permute-start.19 = (bf16[672,256]{1,0:T(8,128)(2,1)S(1)}, bf16[672,256]{1,0:T(8,128)(2,1)S(1)}, u32[]{:S(2)}, u32[]{:S(2)}) collective-permute-start(bf16[672,256]{1,0:T(8,128)(2,1)S(1)} %get-tuple-element.59), channel_id=1, source_target_pairs={{0,56},{4,60},{8,0},{12,4},{16,8},{20,12},{24,16},{28,20},{32,24},... | collective-permute-start | bytes 1032200 | tf_op jit(solution)/shard_map/ppermute | solution.py:38
  86.4 9.9 %collective-permute-start.20 = (bf16[672,256]{1,0:T(8,128)(2,1)S(1)}, bf16[672,256]{1,0:T(8,128)(2,1)S(1)}, u32[]{:S(2)}, u32[]{:S(2)}) collective-permute-start(bf16[672,256]{1,0:T(8,128)(2,1)S(1)} %get-tuple-element.61), channel_id=1, source_target_pairs={{0,8},{4,12},{8,16},{12,20},{16,24},{20,28},{24,32},{28,36},{32,40... | collective-permute-start | bytes 1032200 | tf_op jit(solution)/shard_map/ppermute | solution.py:38
  96.4 2.4 %copy-start.19 = (bf16[272,640]{1,0:T(8,128)(2,1)S(1)}, bf16[272,640]{1,0:T(8,128)(2,1)}, u32[]{:S(2)}) copy-start(bf16[272,640]{1,0:T(8,128)(2,1)} %copy-done.18) | copy-start | bytes 1044484
  96.4 2.4 %copy-start.21 = (bf16[272,640]{1,0:T(8,128)(2,1)S(1)}, bf16[272,640]{1,0:T(8,128)(2,1)}, u32[]{:S(2)}) copy-start(bf16[272,640]{1,0:T(8,128)(2,1)} %copy-done.20) | copy-start | bytes 1044484
  96.6 9.9 %collective-permute-start.21 = (bf16[672,256]{1,0:T(8,128)(2,1)S(1)}, bf16[672,256]{1,0:T(8,128)(2,1)S(1)}, u32[]{:S(2)}, u32[]{:S(2)}) collective-permute-start(bf16[672,256]{1,0:T(8,128)(2,1)S(1)} %get-tuple-element.62), channel_id=1, source_target_pairs={{0,56},{4,60},{8,0},{12,4},{16,8},{20,12},{24,16},{28,20},{32,24},... | collective-permute-start | bytes 1032200 | tf_op jit(solution)/shard_map/ppermute | solution.py:38
  96.7 11.1 %collective-permute-start.22 = (bf16[672,256]{1,0:T(8,128)(2,1)S(1)}, bf16[672,256]{1,0:T(8,128)(2,1)S(1)}, u32[]{:S(2)}, u32[]{:S(2)}) collective-permute-start(bf16[672,256]{1,0:T(8,128)(2,1)S(1)} %get-tuple-element.64), channel_id=1, source_target_pairs={{0,8},{4,12},{8,16},{12,20},{16,24},{20,28},{24,32},{28,36},{32,40... | collective-permute-start | bytes 1032200 | tf_op jit(solution)/shard_map/ppermute | solution.py:38
  107.8 2.4 %copy-start.2 = (bf16[528,640]{1,0:T(8,128)(2,1)S(1)}, bf16[528,640]{1,0:T(8,128)(2,1)}, u32[]{:S(2)}) copy-start(bf16[528,640]{1,0:T(8,128)(2,1)} %copy-done) | copy-start | bytes 2027524
  107.8 2.4 %copy-start.13 = (bf16[272,640]{1,0:T(8,128)(2,1)S(1)}, bf16[272,640]{1,0:T(8,128)(2,1)}, u32[]{:S(2)}) copy-start(bf16[272,640]{1,0:T(8,128)(2,1)} %copy-done.12) | copy-start | bytes 1044484
  108.1 7.3 %collective-permute-start.23 = (bf16[672,256]{1,0:T(8,128)(2,1)S(1)}, bf16[672,256]{1,0:T(8,128)(2,1)S(1)}, u32[]{:S(2)}, u32[]{:S(2)}) collective-permute-start(bf16[672,256]{1,0:T(8,128)(2,1)S(1)} %get-tuple-element.65), channel_id=1, source_target_pairs={{0,56},{4,60},{8,0},{12,4},{16,8},{20,12},{24,16},{28,20},{32,24},... | collective-permute-start | bytes 1032200 | tf_op jit(solution)/shard_map/ppermute | solution.py:38
  108.2 8.5 %collective-permute-start.24 = (bf16[672,256]{1,0:T(8,128)(2,1)S(1)}, bf16[672,256]{1,0:T(8,128)(2,1)S(1)}, u32[]{:S(2)}, u32[]{:S(2)}) collective-permute-start(bf16[672,256]{1,0:T(8,128)(2,1)S(1)} %get-tuple-element.66), channel_id=1, source_target_pairs={{0,8},{4,12},{8,16},{12,20},{16,24},{20,28},{24,32},{28,36},{32,40... | collective-permute-start | bytes 1032200 | tf_op jit(solution)/shard_map/ppermute | solution.py:38
where the time goes:
time: 118 us
  waiting for transfers between devices  36.6 us (31%)
  starting transfers between devices  36.1 us (31%)
  Pallas kernels  27.8 us (24%)
  local copies, waits for them, and re-layouts  16 us (14%)
    ppermute x25, waiting for transfers between devices, move(): return lax.ppermute(array, 'ctx', pairs)  36.6 us
    ppermute x25, starting transfers between devices, move(): return lax.ppermute(array, 'ctx', pairs)  36.1 us
    pallas_call x5, Pallas kernels, part(): pl.pallas_call(functools.partial(part_kernel, heads, groups), in_specs=[s...  26 us
    unnamed x57, local copies, waits for them, and re-layouts  13.3 us
  transfers between devices with their start and end apart: 25, of which 14 were waited for; matrix products, arithmetic and copies ran while one was open for 1% of the time, Pallas kernels for 17%

commit v1 on v0

--- a/solution.py
+++ b/solution.py
@@ -253,7 +253,6 @@
     wanted = FIRST + MOST
     vmem = pl.BlockSpec(memory_space=pltpu.VMEM)
     smem = pl.BlockSpec(memory_space=pltpu.SMEM)
-    hbm = pl.BlockSpec(memory_space=pltpu.HBM)
     widths = [group[2] * BLOCK for group in groups]
     count = len(groups)
     scratch = [pltpu.VMEM((wanted, 2 * BLOCK, columns), jnp.bfloat16)] * count
@@ -270,7 +269,7 @@
     scratch += [pltpu.SemaphoreType.DMA((PLANE,)), pltpu.SemaphoreType.DMA((count,))]
     return pl.pallas_call(
         functools.partial(part_kernel, heads, groups),
-        in_specs=[smem] + [vmem] * count + [hbm] * (2 * PLANE),
+        in_specs=[smem] + [vmem] * (count + 2 * PLANE),
         out_specs=[vmem] * count,
         out_shape=[jax.ShapeDtypeStruct((columns + STATS, w), jnp.bfloat16) for w in widths],
         scratch_shapes=scratch,
@@ -376,18 +375,16 @@
     up1, down1 = move(pay, dz=1), move(pay, dz=-1)
     left, right = move(own, dx=1), move(own, dx=-1)
     own_twin = move(own, dc=1)
-    up1, down1, left, right, own_twin = barrier((up1, down1, left, right, own_twin))
+    up1, down1, left, right = barrier((up1, down1, left, right))
 
     up2, down2 = move(up1, dz=1), move(down1, dz=-1)
     far_k, far_v = move(left[:split], dx=1), move(right[split:], dx=-1)
-    left_twin = move(left, dc=1)
-    up2, down2, far_k, far_v, left_twin = barrier((up2, down2, far_k, far_v, left_twin))
+    up2, down2, far_k, far_v, own_twin = barrier((up2, down2, far_k, far_v, own_twin))
 
     up3, down3 = move(up2, dz=1), move(down2, dz=-1)
-    right_twin, far_k_twin, far_v_twin = move(right, dc=1), move(far_k, dc=1), move(far_v, dc=1)
-    up3, down3, right_twin, far_k_twin, far_v_twin = barrier(
-        (up3, down3, right_twin, far_k_twin, far_v_twin)
-    )
+    left_twin, right_twin = move(left, dc=1), move(right, dc=1)
+    up3, down3, left_twin, right_twin = barrier((up3, down3, left_twin, right_twin))
+    far_k_twin, far_v_twin = move(far_k, dc=1), move(far_v, dc=1)
     far_up = move(up3[: HALF + REQUEST], dz=1)
     far_down = move(down3[HALF:], dz=-1)
 

time: 118 us -> 116 us (0.983); the launches traced: 118 us -> 118 us
  local copies, waits for them, and re-layouts: 16 us -> 7.64 us
  waiting for transfers between devices: 36.6 us -> 41.8 us
  starting transfers between devices: 36.1 us -> 38.7 us
    unnamed x57 -> x39, local copies, waits for them, and re-layouts: 13.3 us -> 4.95 us
    ppermute x25, waiting for transfers between devices: 36.6 us -> 41.8 us  [move(): return lax.ppermute(array, 'ctx', pairs)]
    ppermute x25, starting transfers between devices: 36.1 us -> 38.7 us  [move(): return lax.ppermute(array, 'ctx', pairs)]
  transfers between devices with their start and end apart: 25 -> 25, of which waited for: 14 -> 15; matrix products, arithmetic and copies ran while one was open for 1% -> 1% of each run, Pallas kernels for 17% -> 18%
where the time goes in v1:
time: 116 us; the launch traced here: 118 us
  waiting for transfers between devices  41.8 us (36%)
  starting transfers between devices  38.7 us (33%)
  Pallas kernels  28.5 us (25%)
  local copies, waits for them, and re-layouts  7.64 us (7%)
    ppermute x25, waiting for transfers between devices, move(): return lax.ppermute(array, 'ctx', pairs)  41.8 us
    ppermute x25, starting transfers between devices, move(): return lax.ppermute(array, 'ctx', pairs)  38.7 us
    pallas_call x5, Pallas kernels, part(): pl.pallas_call(functools.partial(part_kernel, heads, groups), in_specs=[s...  26.8 us
    unnamed x39, local copies, waits for them, and re-layouts  4.95 us
  transfers between devices with their start and end apart: 25, of which 15 were waited for; matrix products, arithmetic and copies ran while one was open for 1% of the time, Pallas kernels for 18%

profile of v1, /device:TPU:8, one launch (start us, length us, event | category | flops | bytes accessed | tf_op | source)
XLA Modules:
  0.0 118.0 jit_solution(482923305089704160)
XLA Ops:
  0.0 1.1 fusion.13
  1.1 0.7 convert_bitcast_fusion
  1.8 0.1 copy.10
  1.9 0.8 copy.6
  2.6 0.1 convert_reduce_fusion
  2.7 0.1 convert_reduce_fusion.1
  2.8 0.1 pad_maximum_fusion.rest_1_.rest_9_.rest_2_.rest_10_
  2.9 0.1 fusion.8
  3.0 1.6 %collective-permute-start.2 = (bf16[528,640]{1,0:T(8,128)(2,1)S(1)}, bf16[528,640]{1,0:T(8,128)(2,1)S(1)}, u32[]{:S(2)}, u32[]{:S(2)}) collective-permute-start(bf16[528,640]{1,0:T(8,128)(2,1)S(1)} %pad_maximum_fusion.rest_1_.rest_9_.rest_2_.rest_10_), channel_id=1, source_target_pairs={{0,64},{4,68},{8,72},{12,76},{16,80},{20,84},{24,88},{28,92},{32,9... | collective-permute-start | bytes 2027528 | tf_op jit(solution)/shard_map/ppermute | solution.py:38
  4.6 1.7 %collective-permute-start.3 = (bf16[528,640]{1,0:T(8,128)(2,1)S(1)}, bf16[528,640]{1,0:T(8,128)(2,1)S(1)}, u32[]{:S(2)}, u32[]{:S(2)}) collective-permute-start(bf16[528,640]{1,0:T(8,128)(2,1)S(1)} %pad_maximum_fusion.rest_1_.rest_9_.rest_2_.rest_10_), channel_id=1, source_target_pairs={{0,192},{4,196},{8,200},{12,204},{16,208},{20,212},{24,216},{28,22... | collective-permute-start | bytes 2027528 | tf_op jit(solution)/shard_map/ppermute | solution.py:38
  6.3 1.9 %collective-permute-start = (bf16[272,640]{1,0:T(8,128)(2,1)S(1)}, bf16[272,640]{1,0:T(8,128)(2,1)S(1)}, u32[]{:S(2)}, u32[]{:S(2)}) collective-permute-start(bf16[272,640]{1,0:T(8,128)(2,1)S(1)} %pad_maximum_fusion.1.rest_0_), channel_id=1, source_target_pairs={{0,8},{4,12},{8,16},{12,20},{16,24},{20,28},{24,32},{28,36},{32,40... | collective-permute-start | bytes 1044488 | tf_op jit(solution)/shard_map/ppermute | solution.py:38
  8.3 3.9 %collective-permute-start.1 = (bf16[272,640]{1,0:T(8,128)(2,1)S(1)}, bf16[272,640]{1,0:T(8,128)(2,1)S(1)}, u32[]{:S(2)}, u32[]{:S(2)}) collective-permute-start(bf16[272,640]{1,0:T(8,128)(2,1)S(1)} %pad_maximum_fusion.1.rest_0_), channel_id=1, source_target_pairs={{0,56},{4,60},{8,0},{12,4},{16,8},{20,12},{24,16},{28,20},{32,24},... | collective-permute-start | bytes 1044488 | tf_op jit(solution)/shard_map/ppermute | solution.py:38
  12.2 8.8 %collective-permute-done.rest_0_ = bf16[272,640]{1,0:T(8,128)(2,1)S(1)} collective-permute-done((bf16[272,640]{1,0:T(8,128)(2,1)S(1)}, bf16[272,640]{1,0:T(8,128)(2,1)S(1)}, u32[]{:S(2)}, u32[]{:S(2)}) %collective-permute-start) | collective-permute-done | bytes 348192 | tf_op jit(solution)/shard_map/ppermute | solution.py:38
  21.0 0.2 collective-permute-done.2.rest_7_.rest_15_.rest_8_.rest_16_
  21.3 3.0 %collective-permute-start.7 = (bf16[256,640]{1,0:T(8,128)(2,1)S(1)}, bf16[256,640]{1,0:T(8,128)(2,1)}, u32[]{:S(2)}, u32[]{:S(2)}) collective-permute-start(bf16[256,640]{1,0:T(8,128)(2,1)S(1)} %slice.21), channel_id=1, source_target_pairs={{0,192},{4,196},{8,200},{12,204},{16,208},{20,212},{24,216},{28,22... | collective-permute-start | bytes 983048 | tf_op jit(solution)/shard_map/ppermute | solution.py:38
  24.3 0.0 collective-permute-start.11
  24.3 2.0 %collective-permute-start.4 = (bf16[272,640]{1,0:T(8,128)(2,1)S(1)}, bf16[272,640]{1,0:T(8,128)(2,1)S(1)}, u32[]{:S(2)}, u32[]{:S(2)}) collective-permute-start(bf16[272,640]{1,0:T(8,128)(2,1)S(1)} %collective-permute-done.rest_0_), channel_id=1, source_target_pairs={{0,8},{4,12},{8,16},{12,20},{16,24},{20,28},{24,32},{28,36},{32,40... | collective-permute-start | bytes 1044488 | tf_op jit(solution)/shard_map/ppermute | solution.py:38
  26.3 4.0 %collective-permute-start.5 = (bf16[272,640]{1,0:T(8,128)(2,1)S(1)}, bf16[272,640]{1,0:T(8,128)(2,1)S(1)}, u32[]{:S(2)}, u32[]{:S(2)}) collective-permute-start(bf16[272,640]{1,0:T(8,128)(2,1)S(1)} %collective-permute-done.1.rest_1_), channel_id=1, source_target_pairs={{0,56},{4,60},{8,0},{12,4},{16,8},{20,12},{24,16},{28,20},{32,24},... | collective-permute-start | bytes 1044488 | tf_op jit(solution)/shard_map/ppermute | solution.py:38
  30.4 0.4 collective-permute-done.7.rest_13_.rest_14_
  30.8 8.3 %collective-permute-done.4.rest_0_ = bf16[272,640]{1,0:T(8,128)(2,1)S(1)} collective-permute-done((bf16[272,640]{1,0:T(8,128)(2,1)S(1)}, bf16[272,640]{1,0:T(8,128)(2,1)S(1)}, u32[]{:S(2)}, u32[]{:S(2)}) %collective-permute-start.4) | collective-permute-done | bytes 348192 | tf_op jit(solution)/shard_map/ppermute | solution.py:38
  39.1 0.0 collective-permute-done.5.rest_1_
  39.1 2.9 %collective-permute-done.6.rest_5_.rest_6_ = bf16[272,640]{1,0:T(8,128)(2,1)} collective-permute-done((bf16[272,640]{1,0:T(8,128)(2,1)S(1)}, bf16[272,640]{1,0:T(8,128)(2,1)}, u32[]{:S(2)}, u32[]{:S(2)}) %collective-permute-start.6) | collective-permute-done | bytes 348192 | tf_op jit(solution)/shard_map/ppermute | solution.py:38
  42.0 0.0 collective-permute-start.9
  42.0 0.7 copy-done.13
  42.7 3.2 %collective-permute-start.10 = (bf16[272,640]{1,0:T(8,128)(2,1)S(1)}, bf16[272,640]{1,0:T(8,128)(2,1)S(1)}, u32[]{:S(2)}, u32[]{:S(2)}) collective-permute-start(bf16[272,640]{1,0:T(8,128)(2,1)S(1)} %collective-permute-done.5.rest_1_), channel_id=1, source_target_pairs={{0,56},{4,60},{8,0},{12,4},{16,8},{20,12},{24,16},{28,20},{32,24},... | collective-permute-start | bytes 1044488 | tf_op jit(solution)/shard_map/ppermute | solution.py:38
  45.9 0.7 copy-done.15
  46.7 0.0 collective-permute-start.13
  46.7 0.5 collective-permute-start.14
  47.2 0.9 copy-done
  48.1 4.6 %collective-permute-done.9.rest_0_ = bf16[272,640]{1,0:T(8,128)(2,1)S(1)} collective-permute-done((bf16[272,640]{1,0:T(8,128)(2,1)S(1)}, bf16[272,640]{1,0:T(8,128)(2,1)S(1)}, u32[]{:S(2)}, u32[]{:S(2)}) %collective-permute-start.9) | collective-permute-done | bytes 348192 | tf_op jit(solution)/shard_map/ppermute | solution.py:38
  52.7 0.0 collective-permute-done.10.rest_1_
  52.7 0.7 slice.22
  53.4 0.7 copy-done.5
  54.1 0.5 collective-permute-start.15
  54.6 0.7 slice.23
  55.3 3.2 %collective-permute-start.16 = (bf16[144,640]{1,0:T(8,128)(2,1)}, bf16[144,640]{1,0:T(8,128)(2,1)}, u32[]{:S(2)}, u32[]{:S(2)}) collective-permute-start(bf16[144,640]{1,0:T(8,128)(2,1)} %slice.23), channel_id=1, source_target_pairs={{0,56},{4,60},{8,0},{12,4},{16,8},{20,12},{24,16},{28,20},{32,24},... | collective-permute-start | bytes 552968 | tf_op jit(solution)/shard_map/ppermute | solution.py:38
  58.5 0.1 pad_add_fusion.pos_ref
  58.6 3.0 %collective-permute-done.15.rest_0_ = bf16[144,640]{1,0:T(8,128)(2,1)} collective-permute-done((bf16[144,640]{1,0:T(8,128)(2,1)}, bf16[144,640]{1,0:T(8,128)(2,1)}, u32[]{:S(2)}, u32[]{:S(2)}) %collective-permute-start.15) | collective-permute-done | bytes 184352 | tf_op jit(solution)/shard_map/ppermute | solution.py:38
  61.6 0.2 collective-permute-done.16.rest_1_
  61.9 1.1 copy-done.1
  63.0 6.1 %shard_map.59 = (bf16[672,128]{1,0:T(8,128)(2,1)S(1)}, bf16[672,128]{1,0:T(8,128)(2,1)S(1)}) custom-call(s32[3]{0:T(128)S(1)} %pad_add_fusion.pos_ref, bf16[144,640]{1,0:T(8,128)(2,1)} %collective-permute-done.15.rest_0_, bf16[144,640]{1,0:T(8,128)(2,1)} %collective-permute-done.16.rest_1_, ...), custom_call_target="tpu_custom_call" | custom-call | flops 1342177280 | bytes 4194304 | tf_op jit(solution)/shard_map/pallas_call | solution.py:270
  69.1 6.8 %collective-permute-start.17 = (bf16[672,128]{1,0:T(8,128)(2,1)S(1)}, bf16[672,128]{1,0:T(8,128)(2,1)S(1)}, u32[]{:S(2)}, u32[]{:S(2)}) collective-permute-start(bf16[672,128]{1,0:T(8,128)(2,1)S(1)} %get-tuple-element.52), channel_id=1, source_target_pairs={{0,56},{4,60},{8,0},{12,4},{16,8},{20,12},{24,16},{28,20},{32,24},... | collective-permute-start | bytes 516104 | tf_op jit(solution)/shard_map/ppermute | solution.py:38
  75.8 0.0 collective-permute-start.18
  75.8 5.6 %shard_map.58 = (bf16[672,256]{1,0:T(8,128)(2,1)S(1)}, bf16[672,256]{1,0:T(8,128)(2,1)S(1)}) custom-call(s32[3]{0:T(128)S(1)} %pad_add_fusion.pos_ref, bf16[272,640]{1,0:T(8,128)(2,1)S(1)} %copy-done.6, bf16[272,640]{1,0:T(8,128)(2,1)S(1)} %copy-done.8, bf16[528,640]{1,0:T(8,128)(2,1)S(1)} %pad_maximum_fusion.rest_1_.rest_9_.rest_2_.rest_10_, ...), custom_call_target="tpu_custom_call" | custom-call | flops 1342177280 | bytes 4194304 | tf_op jit(solution)/shard_map/pallas_call | solution.py:270
  81.5 1.2 %collective-permute-done.18.down_in_ref = bf16[672,128]{1,0:T(8,128)(2,1)S(1)} collective-permute-done((bf16[672,128]{1,0:T(8,128)(2,1)S(1)}, bf16[672,128]{1,0:T(8,128)(2,1)S(1)}, u32[]{:S(2)}, u32[]{:S(2)}) %collective-permute-start.18) | collective-permute-done | bytes 172064 | tf_op jit(solution)/shard_map/ppermute | solution.py:38
  82.7 0.2 shard_map.60
  82.9 1.9 %collective-permute-start.19 = (bf16[672,256]{1,0:T(8,128)(2,1)S(1)}, bf16[672,256]{1,0:T(8,128)(2,1)S(1)}, u32[]{:S(2)}, u32[]{:S(2)}) collective-permute-start(bf16[672,256]{1,0:T(8,128)(2,1)S(1)} %get-tuple-element.55), channel_id=1, source_target_pairs={{0,56},{4,60},{8,0},{12,4},{16,8},{20,12},{24,16},{28,20},{32,24},... | collective-permute-start | bytes 1032200 | tf_op jit(solution)/shard_map/ppermute | solution.py:38
  84.8 0.2 collective-permute-start.20
  85.0 5.8 %shard_map.57 = (bf16[672,256]{1,0:T(8,128)(2,1)S(1)}, bf16[672,256]{1,0:T(8,128)(2,1)S(1)}) custom-call(s32[3]{0:T(128)S(1)} %pad_add_fusion.pos_ref, bf16[272,640]{1,0:T(8,128)(2,1)S(1)} %copy-done.14, bf16[272,640]{1,0:T(8,128)(2,1)S(1)} %copy-done.16, bf16[528,640]{1,0:T(8,128)(2,1)S(1)} %pad_maximum_fusion.rest_1_.rest_9_.rest_2_.rest_10_, ...), custom_call_target="tpu_custom_call" | custom-call | flops 1342177280 | bytes 4194304 | tf_op jit(solution)/shard_map/pallas_call | solution.py:270
  90.8 0.9 collective-permute-done.19.up_in_ref
  91.7 4.0 %collective-permute-done.20.down_in_ref = bf16[672,256]{1,0:T(8,128)(2,1)S(1)} collective-permute-done((bf16[672,256]{1,0:T(8,128)(2,1)S(1)}, bf16[672,256]{1,0:T(8,128)(2,1)S(1)}, u32[]{:S(2)}, u32[]{:S(2)}) %collective-permute-start.20) | collective-permute-done | bytes 344096 | tf_op jit(solution)/shard_map/ppermute | solution.py:38
  95.7 0.3 shard_map.61
  95.9 0.1 collective-permute-start.21
  96.0 2.0 %collective-permute-start.22 = (bf16[672,256]{1,0:T(8,128)(2,1)S(1)}, bf16[672,256]{1,0:T(8,128)(2,1)S(1)}, u32[]{:S(2)}, u32[]{:S(2)}) collective-permute-start(bf16[672,256]{1,0:T(8,128)(2,1)S(1)} %get-tuple-element.60), channel_id=1, source_target_pairs={{0,8},{4,12},{8,16},{12,20},{16,24},{20,28},{24,32},{28,36},{32,40... | collective-permute-start | bytes 1032200 | tf_op jit(solution)/shard_map/ppermute | solution.py:38
  98.0 5.6 %shard_map.56 = (bf16[672,256]{1,0:T(8,128)(2,1)S(1)}, bf16[672,256]{1,0:T(8,128)(2,1)S(1)}) custom-call(s32[3]{0:T(128)S(1)} %pad_add_fusion.pos_ref, bf16[272,640]{1,0:T(8,128)(2,1)S(1)} %copy-done.10, bf16[272,640]{1,0:T(8,128)(2,1)S(1)} %copy-done.12, bf16[528,640]{1,0:T(8,128)(2,1)S(1)} %pad_maximum_fusion.rest_1_.rest_9_.rest_2_.rest_10_, ...), custom_call_target="tpu_custom_call" | custom-call | flops 1342177280 | bytes 4194304 | tf_op jit(solution)/shard_map/pallas_call | solution.py:270
  103.6 3.2 %collective-permute-done.21.up_in_ref = bf16[672,256]{1,0:T(8,128)(2,1)S(1)} collective-permute-done((bf16[672,256]{1,0:T(8,128)(2,1)S(1)}, bf16[672,256]{1,0:T(8,128)(2,1)S(1)}, u32[]{:S(2)}, u32[]{:S(2)}) %collective-permute-start.21) | collective-permute-done | bytes 344096 | tf_op jit(solution)/shard_map/ppermute | solution.py:38
  106.8 1.3 %collective-permute-done.22.down_in_ref = bf16[672,256]{1,0:T(8,128)(2,1)S(1)} collective-permute-done((bf16[672,256]{1,0:T(8,128)(2,1)S(1)}, bf16[672,256]{1,0:T(8,128)(2,1)S(1)}, u32[]{:S(2)}, u32[]{:S(2)}) %collective-permute-start.22) | collective-permute-done | bytes 344096 | tf_op jit(solution)/shard_map/ppermute | solution.py:38
  108.1 0.3 shard_map.62
  108.4 0.1 collective-permute-start.23
  108.5 2.0 %collective-permute-start.24 = (bf16[672,256]{1,0:T(8,128)(2,1)S(1)}, bf16[672,256]{1,0:T(8,128)(2,1)S(1)}, u32[]{:S(2)}, u32[]{:S(2)}) collective-permute-start(bf16[672,256]{1,0:T(8,128)(2,1)S(1)} %get-tuple-element.62), channel_id=1, source_target_pairs={{0,8},{4,12},{8,16},{12,20},{16,24},{20,28},{24,32},{28,36},{32,40... | collective-permute-start | bytes 1032200 | tf_op jit(solution)/shard_map/ppermute | solution.py:38
  110.5 3.8 %shard_map.55.own_ref = bf16[672,256]{1,0:T(8,128)(2,1)S(1)} custom-call(s32[3]{0:T(128)S(1)} %pad_add_fusion.pos_ref, bf16[272,640]{1,0:T(8,128)(2,1)S(1)} %copy-done.4, bf16[528,640]{1,0:T(8,128)(2,1)S(1)} %pad_maximum_fusion.rest_1_.rest_9_.rest_2_.rest_10_, bf16[528,640]{1,0:T(8,128)(2,1)S(1)} %collective-permute-done.8.rest_2_.rest_10_.rest_3_.rest_11_, ...), custom_call_target="tpu_custom_call" | custom-call | flops 1342177280 | bytes 4194304 | tf_op jit(solution)/shard_map/pallas_call | solution.py:270
  114.3 1.4 %collective-permute-done.23.up_ref = bf16[672,256]{1,0:T(8,128)(2,1)S(1)} collective-permute-done((bf16[672,256]{1,0:T(8,128)(2,1)S(1)}, bf16[672,256]{1,0:T(8,128)(2,1)S(1)}, u32[]{:S(2)}, u32[]{:S(2)}) %collective-permute-start.23) | collective-permute-done | bytes 344096 | tf_op jit(solution)/shard_map/ppermute | solution.py:38
  115.7 1.3 %collective-permute-done.24.down_ref = bf16[672,256]{1,0:T(8,128)(2,1)S(1)} collective-permute-done((bf16[672,256]{1,0:T(8,128)(2,1)S(1)}, bf16[672,256]{1,0:T(8,128)(2,1)S(1)}, u32[]{:S(2)}, u32[]{:S(2)}) %collective-permute-start.24) | collective-permute-done | bytes 344096 | tf_op jit(solution)/shard_map/ppermute | solution.py:38
  117.0 1.0 shard_map.63
  (49 shorter events, 0.2 us)
Async XLA Ops:
  0.0 2.6 %copy-start.17 = (bf16[256,640]{1,0:T(8,128)(2,1)S(1)}, bf16[256,640]{1,0:T(8,128)(2,1)}, u32[]{:S(2)}) copy-start(bf16[256,640]{1,0:T(8,128)(2,1)} %param.7) | copy-start | bytes 983044
  0.0 2.7 %copy-start.18 = (bf16[256,640]{1,0:T(8,128)(2,1)S(1)}, bf16[256,640]{1,0:T(8,128)(2,1)}, u32[]{:S(2)}) copy-start(bf16[256,640]{1,0:T(8,128)(2,1)} %param.6) | copy-start | bytes 983044
  3.0 21.3 %copy-start.3 = (bf16[272,640]{1,0:T(8,128)(2,1)}, bf16[272,640]{1,0:T(8,128)(2,1)S(1)}, u32[]{:S(2)}) copy-start(bf16[272,640]{1,0:T(8,128)(2,1)S(1)} %pad_maximum_fusion.1.rest_0_) | copy-start | bytes 1044484
  3.0 18.2 %collective-permute-start.2 = (bf16[528,640]{1,0:T(8,128)(2,1)S(1)}, bf16[528,640]{1,0:T(8,128)(2,1)S(1)}, u32[]{:S(2)}, u32[]{:S(2)}) collective-permute-start(bf16[528,640]{1,0:T(8,128)(2,1)S(1)} %pad_maximum_fusion.rest_1_.rest_9_.rest_2_.rest_10_), channel_id=1, source_target_pairs={{0,64},{4,68},{8,72},{12,76},{16,80},{20,84},{24,88},{28,92},{32,9... | collective-permute-start | bytes 2027528 | tf_op jit(solution)/shard_map/ppermute | solution.py:38
  4.6 16.6 %collective-permute-start.3 = (bf16[528,640]{1,0:T(8,128)(2,1)S(1)}, bf16[528,640]{1,0:T(8,128)(2,1)S(1)}, u32[]{:S(2)}, u32[]{:S(2)}) collective-permute-start(bf16[528,640]{1,0:T(8,128)(2,1)S(1)} %pad_maximum_fusion.rest_1_.rest_9_.rest_2_.rest_10_), channel_id=1, source_target_pairs={{0,192},{4,196},{8,200},{12,204},{16,208},{20,212},{24,216},{28,22... | collective-permute-start | bytes 2027528 | tf_op jit(solution)/shard_map/ppermute | solution.py:38
  6.3 24.0 %collective-permute-start.8 = (bf16[528,640]{1,0:T(8,128)(2,1)S(1)}, bf16[528,640]{1,0:T(8,128)(2,1)S(1)}, u32[]{:S(2)}, u32[]{:S(2)}) collective-permute-start(bf16[528,640]{1,0:T(8,128)(2,1)S(1)} %pad_maximum_fusion.rest_1_.rest_9_.rest_2_.rest_10_), channel_id=1, source_target_pairs={{0,4},{4,0},{8,12},{12,8},{16,20},{20,16},{24,28},{28,24},{32,36},... | collective-permute-start | bytes 2027528 | tf_op jit(solution)/shard_map/ppermute | solution.py:38
  6.3 14.7 %collective-permute-start = (bf16[272,640]{1,0:T(8,128)(2,1)S(1)}, bf16[272,640]{1,0:T(8,128)(2,1)S(1)}, u32[]{:S(2)}, u32[]{:S(2)}) collective-permute-start(bf16[272,640]{1,0:T(8,128)(2,1)S(1)} %pad_maximum_fusion.1.rest_0_), channel_id=1, source_target_pairs={{0,8},{4,12},{8,16},{12,20},{16,24},{20,28},{24,32},{28,36},{32,40... | collective-permute-start | bytes 1044488 | tf_op jit(solution)/shard_map/ppermute | solution.py:38
  8.3 12.8 %collective-permute-start.1 = (bf16[272,640]{1,0:T(8,128)(2,1)S(1)}, bf16[272,640]{1,0:T(8,128)(2,1)S(1)}, u32[]{:S(2)}, u32[]{:S(2)}) collective-permute-start(bf16[272,640]{1,0:T(8,128)(2,1)S(1)} %pad_maximum_fusion.1.rest_0_), channel_id=1, source_target_pairs={{0,56},{4,60},{8,0},{12,4},{16,8},{20,12},{24,16},{28,20},{32,24},... | collective-permute-start | bytes 1044488 | tf_op jit(solution)/shard_map/ppermute | solution.py:38
  21.0 3.3 %copy-start.9 = (bf16[272,640]{1,0:T(8,128)(2,1)}, bf16[272,640]{1,0:T(8,128)(2,1)S(1)}, u32[]{:S(2)}) copy-start(bf16[272,640]{1,0:T(8,128)(2,1)S(1)} %collective-permute-done.rest_0_) | copy-start | bytes 1044484
  21.0 5.3 %copy-start.11 = (bf16[272,640]{1,0:T(8,128)(2,1)}, bf16[272,640]{1,0:T(8,128)(2,1)S(1)}, u32[]{:S(2)}) copy-start(bf16[272,640]{1,0:T(8,128)(2,1)S(1)} %collective-permute-done.1.rest_1_) | copy-start | bytes 1044484
  21.3 9.5 %collective-permute-start.7 = (bf16[256,640]{1,0:T(8,128)(2,1)S(1)}, bf16[256,640]{1,0:T(8,128)(2,1)}, u32[]{:S(2)}, u32[]{:S(2)}) collective-permute-start(bf16[256,640]{1,0:T(8,128)(2,1)S(1)} %slice.21), channel_id=1, source_target_pairs={{0,192},{4,196},{8,200},{12,204},{16,208},{20,212},{24,216},{28,22... | collective-permute-start | bytes 983048 | tf_op jit(solution)/shard_map/ppermute | solution.py:38
  24.3 22.4 %collective-permute-start.11 = (bf16[528,640]{1,0:T(8,128)(2,1)S(1)}, bf16[528,640]{1,0:T(8,128)(2,1)S(1)}, u32[]{:S(2)}, u32[]{:S(2)}) collective-permute-start(bf16[528,640]{1,0:T(8,128)(2,1)S(1)} %collective-permute-done.2.rest_7_.rest_15_.rest_8_.rest_16_), channel_id=1, source_target_pairs={{0,4},{4,0},{8,12},{12,8},{16,20},{20,16},{24,28},{28,24},{32,36},... | collective-permute-start | bytes 2027528 | tf_op jit(solution)/shard_map/ppermute | solution.py:38
  24.3 14.8 %collective-permute-start.4 = (bf16[272,640]{1,0:T(8,128)(2,1)S(1)}, bf16[272,640]{1,0:T(8,128)(2,1)S(1)}, u32[]{:S(2)}, u32[]{:S(2)}) collective-permute-start(bf16[272,640]{1,0:T(8,128)(2,1)S(1)} %collective-permute-done.rest_0_), channel_id=1, source_target_pairs={{0,8},{4,12},{8,16},{12,20},{16,24},{20,28},{24,32},{28,36},{32,40... | collective-permute-start | bytes 1044488 | tf_op jit(solution)/shard_map/ppermute | solution.py:38
  26.3 12.8 %collective-permute-start.5 = (bf16[272,640]{1,0:T(8,128)(2,1)S(1)}, bf16[272,640]{1,0:T(8,128)(2,1)S(1)}, u32[]{:S(2)}, u32[]{:S(2)}) collective-permute-start(bf16[272,640]{1,0:T(8,128)(2,1)S(1)} %collective-permute-done.1.rest_1_), channel_id=1, source_target_pairs={{0,56},{4,60},{8,0},{12,4},{16,8},{20,12},{24,16},{28,20},{32,24},... | collective-permute-start | bytes 1044488 | tf_op jit(solution)/shard_map/ppermute | solution.py:38
  30.4 11.6 %collective-permute-start.6 = (bf16[272,640]{1,0:T(8,128)(2,1)S(1)}, bf16[272,640]{1,0:T(8,128)(2,1)}, u32[]{:S(2)}, u32[]{:S(2)}) collective-permute-start(bf16[272,640]{1,0:T(8,128)(2,1)S(1)} %slice.20), channel_id=1, source_target_pairs={{0,64},{4,68},{8,72},{12,76},{16,80},{20,84},{24,88},{28,92},{32,9... | collective-permute-start | bytes 1044488 | tf_op jit(solution)/shard_map/ppermute | solution.py:38
  30.8 16.4 %collective-permute-start.12 = (bf16[528,640]{1,0:T(8,128)(2,1)S(1)}, bf16[528,640]{1,0:T(8,128)(2,1)S(1)}, u32[]{:S(2)}, u32[]{:S(2)}) collective-permute-start(bf16[528,640]{1,0:T(8,128)(2,1)S(1)} %collective-permute-done.3.rest_3_.rest_11_.rest_4_.rest_12_), channel_id=1, source_target_pairs={{0,4},{4,0},{8,12},{12,8},{16,20},{20,16},{24,28},{28,24},{32,36},... | collective-permute-start | bytes 2027528 | tf_op jit(solution)/shard_map/ppermute | solution.py:38
  42.0 10.7 %collective-permute-start.9 = (bf16[272,640]{1,0:T(8,128)(2,1)S(1)}, bf16[272,640]{1,0:T(8,128)(2,1)S(1)}, u32[]{:S(2)}, u32[]{:S(2)}) collective-permute-start(bf16[272,640]{1,0:T(8,128)(2,1)S(1)} %collective-permute-done.4.rest_0_), channel_id=1, source_target_pairs={{0,8},{4,12},{8,16},{12,20},{16,24},{20,28},{24,32},{28,36},{32,40... | collective-permute-start | bytes 1044488 | tf_op jit(solution)/shard_map/ppermute | solution.py:38
  42.0 0.7 copy-start.13
  42.7 9.9 %collective-permute-start.10 = (bf16[272,640]{1,0:T(8,128)(2,1)S(1)}, bf16[272,640]{1,0:T(8,128)(2,1)S(1)}, u32[]{:S(2)}, u32[]{:S(2)}) collective-permute-start(bf16[272,640]{1,0:T(8,128)(2,1)S(1)} %collective-permute-done.5.rest_1_), channel_id=1, source_target_pairs={{0,56},{4,60},{8,0},{12,4},{16,8},{20,12},{24,16},{28,20},{32,24},... | collective-permute-start | bytes 1044488 | tf_op jit(solution)/shard_map/ppermute | solution.py:38
  45.9 0.7 copy-start.15
  46.7 11.9 %collective-permute-start.13 = (bf16[272,640]{1,0:T(8,128)(2,1)}, bf16[272,640]{1,0:T(8,128)(2,1)}, u32[]{:S(2)}, u32[]{:S(2)}) collective-permute-start(bf16[272,640]{1,0:T(8,128)(2,1)} %collective-permute-done.6.rest_5_.rest_6_), channel_id=1, source_target_pairs={{0,4},{4,0},{8,12},{12,8},{16,20},{20,16},{24,28},{28,24},{32,36},... | collective-permute-start | bytes 1044488 | tf_op jit(solution)/shard_map/ppermute | solution.py:38
  46.7 11.9 %collective-permute-start.14 = (bf16[256,640]{1,0:T(8,128)(2,1)}, bf16[256,640]{1,0:T(8,128)(2,1)}, u32[]{:S(2)}, u32[]{:S(2)}) collective-permute-start(bf16[256,640]{1,0:T(8,128)(2,1)} %collective-permute-done.7.rest_13_.rest_14_), channel_id=1, source_target_pairs={{0,4},{4,0},{8,12},{12,8},{16,20},{20,16},{24,28},{28,24},{32,36},... | collective-permute-start | bytes 983048 | tf_op jit(solution)/shard_map/ppermute | solution.py:38
  47.2 0.9 copy-start
  52.7 2.0 %copy-start.7 = (bf16[272,640]{1,0:T(8,128)(2,1)}, bf16[272,640]{1,0:T(8,128)(2,1)S(1)}, u32[]{:S(2)}) copy-start(bf16[272,640]{1,0:T(8,128)(2,1)S(1)} %collective-permute-done.10.rest_1_) | copy-start | bytes 1044484
  53.4 0.7 copy-start.5
  54.1 7.5 %collective-permute-start.15 = (bf16[144,640]{1,0:T(8,128)(2,1)}, bf16[144,640]{1,0:T(8,128)(2,1)}, u32[]{:S(2)}, u32[]{:S(2)}) collective-permute-start(bf16[144,640]{1,0:T(8,128)(2,1)} %slice.22), channel_id=1, source_target_pairs={{0,8},{4,12},{8,16},{12,20},{16,24},{20,28},{24,32},{28,36},{32,40... | collective-permute-start | bytes 552968 | tf_op jit(solution)/shard_map/ppermute | solution.py:38
  55.3 6.6 %collective-permute-start.16 = (bf16[144,640]{1,0:T(8,128)(2,1)}, bf16[144,640]{1,0:T(8,128)(2,1)}, u32[]{:S(2)}, u32[]{:S(2)}) collective-permute-start(bf16[144,640]{1,0:T(8,128)(2,1)} %slice.23), channel_id=1, source_target_pairs={{0,56},{4,60},{8,0},{12,4},{16,8},{20,12},{24,16},{28,20},{32,24},... | collective-permute-start | bytes 552968 | tf_op jit(solution)/shard_map/ppermute | solution.py:38
  61.9 1.1 copy-start.1
  63.0 12.9 %copy-start.6 = (bf16[272,640]{1,0:T(8,128)(2,1)S(1)}, bf16[272,640]{1,0:T(8,128)(2,1)}, u32[]{:S(2)}) copy-start(bf16[272,640]{1,0:T(8,128)(2,1)} %copy-done.5) | copy-start | bytes 1044484
  63.0 12.9 %copy-start.8 = (bf16[272,640]{1,0:T(8,128)(2,1)S(1)}, bf16[272,640]{1,0:T(8,128)(2,1)}, u32[]{:S(2)}) copy-start(bf16[272,640]{1,0:T(8,128)(2,1)} %copy-done.7) | copy-start | bytes 1044484
  69.1 12.4 %collective-permute-start.17 = (bf16[672,128]{1,0:T(8,128)(2,1)S(1)}, bf16[672,128]{1,0:T(8,128)(2,1)S(1)}, u32[]{:S(2)}, u32[]{:S(2)}) collective-permute-start(bf16[672,128]{1,0:T(8,128)(2,1)S(1)} %get-tuple-element.52), channel_id=1, source_target_pairs={{0,56},{4,60},{8,0},{12,4},{16,8},{20,12},{24,16},{28,20},{32,24},... | collective-permute-start | bytes 516104 | tf_op jit(solution)/shard_map/ppermute | solution.py:38
  75.8 6.8 %collective-permute-start.18 = (bf16[672,128]{1,0:T(8,128)(2,1)S(1)}, bf16[672,128]{1,0:T(8,128)(2,1)S(1)}, u32[]{:S(2)}, u32[]{:S(2)}) collective-permute-start(bf16[672,128]{1,0:T(8,128)(2,1)S(1)} %get-tuple-element.54), channel_id=1, source_target_pairs={{0,8},{4,12},{8,16},{12,20},{16,24},{20,28},{24,32},{28,36},{32,40... | collective-permute-start | bytes 516104 | tf_op jit(solution)/shard_map/ppermute | solution.py:38
  81.4 3.6 %copy-start.14 = (bf16[272,640]{1,0:T(8,128)(2,1)S(1)}, bf16[272,640]{1,0:T(8,128)(2,1)}, u32[]{:S(2)}) copy-start(bf16[272,640]{1,0:T(8,128)(2,1)} %copy-done.13) | copy-start | bytes 1044484
  81.4 3.6 %copy-start.16 = (bf16[272,640]{1,0:T(8,128)(2,1)S(1)}, bf16[272,640]{1,0:T(8,128)(2,1)}, u32[]{:S(2)}) copy-start(bf16[272,640]{1,0:T(8,128)(2,1)} %copy-done.15) | copy-start | bytes 1044484
  82.9 8.8 %collective-permute-start.19 = (bf16[672,256]{1,0:T(8,128)(2,1)S(1)}, bf16[672,256]{1,0:T(8,128)(2,1)S(1)}, u32[]{:S(2)}, u32[]{:S(2)}) collective-permute-start(bf16[672,256]{1,0:T(8,128)(2,1)S(1)} %get-tuple-element.55), channel_id=1, source_target_pairs={{0,56},{4,60},{8,0},{12,4},{16,8},{20,12},{24,16},{28,20},{32,24},... | collective-permute-start | bytes 1032200 | tf_op jit(solution)/shard_map/ppermute | solution.py:38
  84.8 10.8 %collective-permute-start.20 = (bf16[672,256]{1,0:T(8,128)(2,1)S(1)}, bf16[672,256]{1,0:T(8,128)(2,1)S(1)}, u32[]{:S(2)}, u32[]{:S(2)}) collective-permute-start(bf16[672,256]{1,0:T(8,128)(2,1)S(1)} %get-tuple-element.57), channel_id=1, source_target_pairs={{0,8},{4,12},{8,16},{12,20},{16,24},{20,28},{24,32},{28,36},{32,40... | collective-permute-start | bytes 1032200 | tf_op jit(solution)/shard_map/ppermute | solution.py:38
  95.7 2.4 %copy-start.10 = (bf16[272,640]{1,0:T(8,128)(2,1)S(1)}, bf16[272,640]{1,0:T(8,128)(2,1)}, u32[]{:S(2)}) copy-start(bf16[272,640]{1,0:T(8,128)(2,1)} %copy-done.9) | copy-start | bytes 1044484
  95.7 2.4 %copy-start.12 = (bf16[272,640]{1,0:T(8,128)(2,1)S(1)}, bf16[272,640]{1,0:T(8,128)(2,1)}, u32[]{:S(2)}) copy-start(bf16[272,640]{1,0:T(8,128)(2,1)} %copy-done.11) | copy-start | bytes 1044484
  95.9 10.8 %collective-permute-start.21 = (bf16[672,256]{1,0:T(8,128)(2,1)S(1)}, bf16[672,256]{1,0:T(8,128)(2,1)S(1)}, u32[]{:S(2)}, u32[]{:S(2)}) collective-permute-start(bf16[672,256]{1,0:T(8,128)(2,1)S(1)} %get-tuple-element.58), channel_id=1, source_target_pairs={{0,56},{4,60},{8,0},{12,4},{16,8},{20,12},{24,16},{28,20},{32,24},... | collective-permute-start | bytes 1032200 | tf_op jit(solution)/shard_map/ppermute | solution.py:38
  96.0 12.0 %collective-permute-start.22 = (bf16[672,256]{1,0:T(8,128)(2,1)S(1)}, bf16[672,256]{1,0:T(8,128)(2,1)S(1)}, u32[]{:S(2)}, u32[]{:S(2)}) collective-permute-start(bf16[672,256]{1,0:T(8,128)(2,1)S(1)} %get-tuple-element.60), channel_id=1, source_target_pairs={{0,8},{4,12},{8,16},{12,20},{16,24},{20,28},{24,32},{28,36},{32,40... | collective-permute-start | bytes 1032200 | tf_op jit(solution)/shard_map/ppermute | solution.py:38
  108.1 2.4 %copy-start.2 = (bf16[528,640]{1,0:T(8,128)(2,1)S(1)}, bf16[528,640]{1,0:T(8,128)(2,1)}, u32[]{:S(2)}) copy-start(bf16[528,640]{1,0:T(8,128)(2,1)} %copy-done) | copy-start | bytes 2027524
  108.1 2.4 %copy-start.4 = (bf16[272,640]{1,0:T(8,128)(2,1)S(1)}, bf16[272,640]{1,0:T(8,128)(2,1)}, u32[]{:S(2)}) copy-start(bf16[272,640]{1,0:T(8,128)(2,1)} %copy-done.3) | copy-start | bytes 1044484
  108.4 7.3 %collective-permute-start.23 = (bf16[672,256]{1,0:T(8,128)(2,1)S(1)}, bf16[672,256]{1,0:T(8,128)(2,1)S(1)}, u32[]{:S(2)}, u32[]{:S(2)}) collective-permute-start(bf16[672,256]{1,0:T(8,128)(2,1)S(1)} %get-tuple-element.61), channel_id=1, source_target_pairs={{0,56},{4,60},{8,0},{12,4},{16,8},{20,12},{24,16},{28,20},{32,24},... | collective-permute-start | bytes 1032200 | tf_op jit(solution)/shard_map/ppermute | solution.py:38
  108.5 8.5 %collective-permute-start.24 = (bf16[672,256]{1,0:T(8,128)(2,1)S(1)}, bf16[672,256]{1,0:T(8,128)(2,1)S(1)}, u32[]{:S(2)}, u32[]{:S(2)}) collective-permute-start(bf16[672,256]{1,0:T(8,128)(2,1)S(1)} %get-tuple-element.62), channel_id=1, source_target_pairs={{0,8},{4,12},{8,16},{12,20},{16,24},{20,28},{24,32},{28,36},{32,40... | collective-permute-start | bytes 1032200 | tf_op jit(solution)/shard_map/ppermute | solution.py:38
